TPU v7x, 256 devices: a whole 4x4x8 slice. The times are simulated.
256 devices in a mesh: fsdp: 2 (over y_hi), rows: 16 (over z, core), cols: 8 (over y_lo, x).
Axes of the slice: x: 4, y: 4 (y_hi: 2, y_lo: 2; y = y_hi * 2 + y_lo), z: 8, core: 2. Of those that a mesh axis runs over, the one named last changes fastest.
Arguments:
- image: bfloat16 [2, 256, 1024, 128], P('fsdp', 'rows', 'cols'), may hold values from -6 to 6
- dw_kernel: float32 [7, 7, 128], replicated, may hold values from -0.875 to 0.875
- dw_bias: float32 [128], replicated, may hold values from -3 to 3
- layer_norm_gain: float32 [128], replicated, may hold values from 0.1 to 1.9
- layer_norm_bias: float32 [128], replicated, may hold values from -3 to 3
- w_in: bfloat16 [128, 512], P('fsdp'), may hold values from -0.5 to 0.5
- b_in: float32 [512], replicated, may hold values from -3 to 3
- w_out: bfloat16 [512, 128], P('fsdp'), may hold values from -0.25 to 0.25
- b_out: float32 [128], replicated, may hold values from -3 to 3
- cotangent: bfloat16 [2, 256, 1024, 128], P('fsdp', 'rows', 'cols'), may hold values from -60 to 60
Outputs:
- mixed: bfloat16 [2, 256, 1024, 128], P('fsdp', 'rows', 'cols')
- d_image: bfloat16 [2, 256, 1024, 128], P('fsdp', 'rows', 'cols')
- g_w_in: float32 [128, 512], P('fsdp')
- g_w_out: float32 [512, 128], P('fsdp')
- g_b_in: float32 [512], replicated
- g_kernel: float32 [7, 7, 128], replicated
- g_gain: float32 [128], replicated
All inputs are finite; a program needn't handle non-finite values.
Results may differ from a plain program's by a relative error of at most 0.0057.
Values may be sent and summed in bfloat16 or wider, within the bound.
A program may use at most 64 MiB of HBM per device.

v0:
```python
import math

import jax
import jax.numpy as jnp
from jax import lax
from jax.sharding import PartitionSpec as P

norm_eps = 1e-06
gelu_coef = math.sqrt(2.0 / math.pi)
cubic_coef = 0.044715


def padded_2(shard, sides, width):
    for axis, dim in sides:
        devices, length = (lax.axis_size(axis), shard.shape[dim])
        up = [(i, (i + 1) % devices) for i in range(devices - 1)]
        down = [(j, i) for i, j in up]
        last = lax.slice_in_dim(shard, length - width, length, axis=dim)
        leading = lax.slice_in_dim(shard, 0, width, axis=dim)
        before = lax.ppermute(last, axis, up)
        after = lax.ppermute(leading, axis, down)
        shard = jnp.concatenate([before, shard, after], axis=dim)
    return shard


def depthwise_taps(padded, kernel, height, width):
    total = jnp.zeros((height, width, padded.shape[2]), jnp.float32)
    for row_tap in range(7):
        for col_tap in range(7):
            total = (
                total
                + padded[row_tap : row_tap + height, col_tap : col_tap + width]
                * kernel[row_tap, col_tap]
            )
    return total


def transposed_taps(padded, kernel, height, width):
    total = jnp.zeros((height, width, padded.shape[2]), jnp.float32)
    for row_tap in range(7):
        for col_tap in range(7):
            total = (
                total
                + padded[6 - row_tap : 6 - row_tap + height, 6 - col_tap : 6 - col_tap + width]
                * kernel[row_tap, col_tap]
            )
    return total


def gelu_parts(pre):
    inner = gelu_coef * (pre + cubic_coef * pre * pre * pre)
    tanh_val = jnp.tanh(inner)
    value = 0.5 * pre * (1.0 + tanh_val)
    slope = 0.5 * (1.0 + tanh_val) + 0.5 * pre * (1.0 - tanh_val * tanh_val) * gelu_coef * (
        1.0 + 3.0 * cubic_coef * pre * pre
    )
    return (value, slope)


def extend_image(field):
    return padded_2(field, (("rows", 0), ("cols", 1)), 3)


def extend_grad(field):
    return padded_2(field, (("rows", 0), ("cols", 1)), 3)


def on_device(
    image, dw_kernel, dw_bias, layer_norm_gain, layer_norm_bias, w_in, b_in, w_out, b_out, cotangent
):
    contract_rows = (((0,), (0,)), ((), ()))
    contract_cols = (((1,), (1,)), ((), ()))
    field = image[0]
    upstream = cotangent[0]
    height, width, channel_count = field.shape
    padded_f = extend_image(field).astype(jnp.float32)
    conv = depthwise_taps(padded_f, dw_kernel, height, width) + dw_bias
    center = jnp.mean(conv, axis=-1, keepdims=True)
    variance_spread = conv - center
    inverse_deviation = lax.rsqrt(
        jnp.mean(variance_spread * variance_spread, axis=-1, keepdims=True) + norm_eps
    )
    standardized_input = variance_spread * inverse_deviation
    normalized_input = (
        (standardized_input * layer_norm_gain + layer_norm_bias)
        .astype(jnp.bfloat16)
        .reshape(-1, channel_count)
    )
    full_in, full_out = (
        lax.all_gather(w_in, "fsdp", axis=0, tiled=True),
        lax.all_gather(w_out, "fsdp", axis=0, tiled=True),
    )
    pre = jnp.dot(normalized_input, full_in, preferred_element_type=jnp.float32) + b_in
    value, slope = gelu_parts(pre)
    hidden = value.astype(jnp.bfloat16)
    mixed = (
        field.reshape(-1, channel_count).astype(jnp.float32)
        + jnp.dot(hidden, full_out, preferred_element_type=jnp.float32)
        + b_out
    )
    mixed = mixed.astype(jnp.bfloat16).reshape(height, width, channel_count)
    flat_up = upstream.reshape(-1, channel_count)
    d_hidden = lax.dot_general(flat_up, full_out, contract_cols, preferred_element_type=jnp.float32)
    d_pre = (d_hidden * slope).astype(jnp.bfloat16)
    normalized_gradient = lax.dot_general(
        d_pre, full_in, contract_cols, preferred_element_type=jnp.float32
    ).reshape(height, width, channel_count)
    gain_product = jnp.sum(normalized_gradient * standardized_input, axis=(0, 1))
    centered_scaled_gradient = normalized_gradient * layer_norm_gain
    convolution_gradient = (
        inverse_deviation
        * (
            centered_scaled_gradient
            - jnp.mean(centered_scaled_gradient, axis=-1, keepdims=True)
            - standardized_input
            * jnp.mean(centered_scaled_gradient * standardized_input, axis=-1, keepdims=True)
        )
    ).astype(jnp.bfloat16)
    bias_term = jnp.sum(d_pre.astype(jnp.float32), axis=0)
    grad_padded = extend_grad(convolution_gradient).astype(jnp.float32)
    d_image = (
        upstream.astype(jnp.float32) + transposed_taps(grad_padded, dw_kernel, height, width)
    ).astype(jnp.bfloat16)
    conv_grad = convolution_gradient.astype(jnp.float32)
    kernel_rows = []
    for row_tap in range(7):
        for col_tap in range(7):
            kernel_rows.append(
                jnp.sum(
                    padded_f[row_tap : row_tap + height, col_tap : col_tap + width] * conv_grad,
                    axis=(0, 1),
                )
            )
    kernel_term = jnp.stack(kernel_rows).reshape(7, 7, channel_count)
    in_rows = w_in.shape[0]
    out_rows = w_out.shape[0]
    term_in = lax.dot_general(
        normalized_input, d_pre, contract_rows, preferred_element_type=jnp.float32
    )
    term_out = lax.dot_general(hidden, flat_up, contract_rows, preferred_element_type=jnp.float32)
    total_in, total_out, g_b_in, g_kernel, g_gain = lax.psum(
        (term_in, term_out, bias_term, kernel_term, gain_product), ("fsdp", "rows", "cols")
    )
    owner = lax.axis_index("fsdp")
    g_w_in = lax.dynamic_slice_in_dim(total_in, owner * in_rows, in_rows, 0)
    g_w_out = lax.dynamic_slice_in_dim(total_out, owner * out_rows, out_rows, 0)
    return (mixed[None], d_image[None], g_w_in, g_w_out, g_b_in, g_kernel, g_gain)


def solution(mesh):
    return jax.shard_map(
        on_device,
        mesh=mesh,
        in_specs=(
            P("fsdp", "rows", "cols", None),
            P(),
            P(),
            P(),
            P(),
            P("fsdp", None),
            P(),
            P("fsdp", None),
            P(),
            P("fsdp", "rows", "cols", None),
        ),
        out_specs=(
            P("fsdp", "rows", "cols", None),
            P("fsdp", "rows", "cols", None),
            P("fsdp", None),
            P("fsdp", None),
            P(),
            P(),
            P(),
        ),
        check_vma=False,
    )
```

profile of v0, /device:TPU:1, one launch (start us, length us, event | category | flops | bytes accessed | tf_op | source)
XLA Modules:
  0.0 337.1 jit_solution(13546384740173514943)
XLA Ops:
  7.2 1.0 slice_bitcast_fusion.1
  8.2 4.9 %collective-permute-start = (bf16[3,128,128]{2,1,0:T(8,128)(2,1)S(1)}, bf16[3,128,128]{2,1,0:T(8,128)(2,1)S(1)}, u32[]{:S(2)}, u32[]{:S(2)}) collective-permute-start(bf16[3,128,128]{2,1,0:T(8,128)(2,1)S(1)} %get-tuple-element.72), channel_id=1, source_target_pairs={{0,8},{8,16},{16,24},{24,32},{32,40},{40,48},{48,56},{56,64},{64,7... | collective-permute-start | bytes 294920 | tf_op jit(solution)/shard_map/ppermute | solution.py:20
  13.1 1.9 collective-permute-start.1
  15.0 1.0 slice_bitcast_fusion.49
  16.1 1.0 slice_bitcast_fusion.50
  17.0 0.9 slice_bitcast_fusion.48
  17.9 5.6 %all_gather.6 = bf16[128,512]{1,0:T(8,128)(2,1)S(1)} all-gather(bf16[64,512]{1,0:T(8,128)(2,1)} %param.15), channel_id=1, replica_groups=mesh['fsdp'=2,'rows'=16,'cols'=8] {'fsdp'}, dimensions={0}, use_global_device_ids=true | all-gather | bytes 196608 | tf_op jit(solution)/shard_map/all_gather | solution.py:90
  23.6 0.8 pad_maximum_fusion.5
  24.4 3.0 collective-permute-start.2
  27.4 1.3 collective-permute-start.3
  28.7 6.1 %all_gather.7 = bf16[512,128]{1,0:T(8,128)(2,1)S(1)} all-gather(bf16[256,128]{1,0:T(8,128)(2,1)} %param.17), channel_id=1, replica_groups=mesh['fsdp'=2,'rows'=16,'cols'=8] {'fsdp'}, dimensions={0}, use_global_device_ids=true | all-gather | bytes 196608 | tf_op jit(solution)/shard_map/all_gather | solution.py:91
  34.8 1.3 maximum_convert_fusion
  36.1 8.2 %fusion.109 = (f32[16,128]{1,0:T(8,128)S(1)}, f32[16,128,128]{2,1,0:T(8,128)S(1)}) fusion(f32[128]{0:T(128)} %param.12, f32[128]{0:T(128)S(1)} %get-tuple-element.121, f32[22,134,128]{2,1,0:T(8,128)S(1)} %maximum_convert_fusion, f32[128]{0:T(128)S(1)} %get-tuple-element.122, f32[128]{0:T(128)S(1)} %get-tuple-element.75, f32[128]{0:T(128)S(1)} %get-tuple-element.76, ...), kind=kLoop, calls=%fused_computation.285 | loop fusion | flops 25950208 | bytes 52462592 | tf_op jit(solution)/shard_map/reduce_sum | solution.py:78
  45.7 1.8 multiply_convert_fusion
  47.5 3.1 convert_reduce_fusion
  51.4 1.0 multiply_reduce_fusion
  52.5 3.0 fusion.56
  55.5 2.4 fusion.57
  57.9 1.7 fusion.55
  59.6 1.2 fusion.111
  60.8 5.6 %collective-permute-start.4 = (bf16[3,128,128]{2,1,0:T(8,128)(2,1)S(1)}, bf16[3,128,128]{2,1,0:T(8,128)(2,1)S(1)}, u32[]{:S(2)}, u32[]{:S(2)}) collective-permute-start(bf16[3,128,128]{2,1,0:T(8,128)(2,1)S(1)} %get-tuple-element.70), channel_id=1, source_target_pairs={{0,8},{8,16},{16,24},{24,32},{32,40},{40,48},{48,56},{56,64},{64,7... | collective-permute-start | bytes 294920 | tf_op jit(solution)/shard_map/ppermute | solution.py:20
  66.4 1.9 collective-permute-start.5
  68.4 1.5 fusion.112
  69.9 2.5 collective-permute-done.5
  72.4 4.3 %collective-permute-start.6 = (bf16[22,3,128]{2,1,0:T(4,128)(2,1)S(1)}, bf16[22,3,128]{2,1,0:T(4,128)(2,1)S(1)}, u32[]{:S(2)}, u32[]{:S(2)}) collective-permute-start(bf16[22,3,128]{2,1,0:T(4,128)(2,1)S(1)} %get-tuple-element.66), channel_id=1, source_target_pairs={{0,1},{1,2},{2,3},{3,4},{4,5},{5,6},{6,7},{8,9},{9,10},{10,11},{11... | collective-permute-start | bytes 50696 | tf_op jit(solution)/shard_map/ppermute | solution.py:20
  76.7 1.5 collective-permute-start.7
  78.2 3.1 fusion.8
  81.4 85.8 %all-reduce = (f32[512]{0:T(512)}, f32[7,7,128]{2,1,0:T(8,128)}, f32[128]{0:T(128)}) all-reduce(f32[512]{0:T(512)S(1)} %get-tuple-element.127, f32[7,7,128]{2,1,0:T(8,128)S(1)} %reshape.62, f32[128]{0:T(128)S(1)} %get-tuple-element.56), channel_id=1, replica_groups=mesh['fsdp'=2,'rows'=16,'cols'=8] {'fsdp','rows','cols'}, use_global_device_ids=true, to_apply=%region_7.0 | all-reduce | flops 6912 | bytes 55296 | tf_op jit(solution)/shard_map/psum | solution.py:141
  167.5 8.1 %fusion.108 = bf16[1,16,128,128]{3,2,1,0:T(8,128)(2,1)} fusion(f32[128]{0:T(128)S(1)} %get-tuple-element.121, f32[22,134,128]{2,1,0:T(8,128)S(1)} %maximum_convert_fusion.1, f32[128]{0:T(128)S(1)} %get-tuple-element.122, f32[128]{0:T(128)S(1)} %get-tuple-element.75, f32[128]{0:T(128)S(1)} %get-tuple-element.76, f32[128]{0:T(128)S(1)} %get-tuple-element.77, ...), kind=kLoop, calls=%fused_computation.221 | loop fusion | flops 26214400 | bytes 52453888 | tf_op jit(solution)/shard_map/broadcast_in_dim | solution.py:147
  175.6 151.5 %all-reduce.4.cloned.1.call-done = (f32[128,512]{1,0:T(8,128)}, f32[512,128]{1,0:T(8,128)}) async-done(((f32[128,512]{1,0:T(8,128)}, f32[512,128]{1,0:T(8,128)}), (f32[128,512]{1,0:T(8,128)}, f32[512,128]{1,0:T(8,128)})) %all-reduce.4.cloned.1.call-update) | async-done | bytes 524304 | tf_op jit(solution)/shard_map/psum | solution.py:141
  327.1 1.6 constant_dynamic-slice_fusion
  328.7 1.6 constant_dynamic-slice_fusion.1
  (37 shorter events, 2.6 us)
Async XLA Ops:
  7.2 319.9 %all-reduce.4.cloned.1.call-start = ((), (), s32[]{:S(2)}) async-start(), calls=%async_computation | async-start | bytes 1048576 | tf_op jit(solution)/shard_map/psum | solution.py:141
  8.2 15.4 %collective-permute-start = (bf16[3,128,128]{2,1,0:T(8,128)(2,1)S(1)}, bf16[3,128,128]{2,1,0:T(8,128)(2,1)S(1)}, u32[]{:S(2)}, u32[]{:S(2)}) collective-permute-start(bf16[3,128,128]{2,1,0:T(8,128)(2,1)S(1)} %get-tuple-element.72), channel_id=1, source_target_pairs={{0,8},{8,16},{16,24},{24,32},{32,40},{40,48},{48,56},{56,64},{64,7... | collective-permute-start | bytes 294920 | tf_op jit(solution)/shard_map/ppermute | solution.py:20
  13.1 10.5 %collective-permute-start.1 = (bf16[3,128,128]{2,1,0:T(8,128)(2,1)S(1)}, bf16[3,128,128]{2,1,0:T(8,128)(2,1)S(1)}, u32[]{:S(2)}, u32[]{:S(2)}) collective-permute-start(bf16[3,128,128]{2,1,0:T(8,128)(2,1)S(1)} %get-tuple-element.73), channel_id=1, source_target_pairs={{8,0},{16,8},{24,16},{32,24},{40,32},{48,40},{56,48},{64,56},{72,6... | collective-permute-start | bytes 294920 | tf_op jit(solution)/shard_map/ppermute | solution.py:21
  24.4 10.4 %collective-permute-start.2 = (bf16[22,3,128]{2,1,0:T(4,128)(2,1)S(1)}, bf16[22,3,128]{2,1,0:T(4,128)(2,1)S(1)}, u32[]{:S(2)}, u32[]{:S(2)}) collective-permute-start(bf16[22,3,128]{2,1,0:T(4,128)(2,1)S(1)} %get-tuple-element.68), channel_id=1, source_target_pairs={{0,1},{1,2},{2,3},{3,4},{4,5},{5,6},{6,7},{8,9},{9,10},{10,11},{11... | collective-permute-start | bytes 50696 | tf_op jit(solution)/shard_map/ppermute | solution.py:20
  27.4 7.4 %collective-permute-start.3 = (bf16[22,3,128]{2,1,0:T(4,128)(2,1)S(1)}, bf16[22,3,128]{2,1,0:T(4,128)(2,1)S(1)}, u32[]{:S(2)}, u32[]{:S(2)}) collective-permute-start(bf16[22,3,128]{2,1,0:T(4,128)(2,1)S(1)} %get-tuple-element.69), channel_id=1, source_target_pairs={{1,0},{2,1},{3,2},{4,3},{5,4},{6,5},{7,6},{9,8},{10,9},{11,10},{12... | collective-permute-start | bytes 50696 | tf_op jit(solution)/shard_map/ppermute | solution.py:21
  36.1 8.9 %copy-start.4 = (f32[128]{0:T(128)S(1)}, f32[128]{0:T(128)}, u32[]{:S(2)}) copy-start(f32[128]{0:T(128)} %param.13) | copy-start | bytes 1540
  36.1 8.9 %copy-start.5 = (f32[128]{0:T(128)S(1)}, f32[128]{0:T(128)}, u32[]{:S(2)}) copy-start(f32[128]{0:T(128)} %param.14) | copy-start | bytes 1540
  36.1 9.5 %copy-start.7 = (f32[512]{0:T(512)S(1)}, f32[512]{0:T(512)}, u32[]{:S(2)}) copy-start(f32[512]{0:T(512)} %param.16) | copy-start | bytes 6148
  45.7 1.8 copy-start.2
  47.5 20.9 %copy-start = (bf16[2048,512]{1,0:T(8,128)(2,1)}, bf16[2048,512]{1,0:T(8,128)(2,1)S(1)}, u32[]{:S(2)}) copy-start(bf16[2048,512]{1,0:T(8,128)(2,1)S(1)} %get-tuple-element.123) | copy-start | bytes 6291460
  59.6 18.6 %copy-start.1 = (bf16[1,16,128,128]{3,2,1,0:T(8,128)(2,1)S(1)}, bf16[1,16,128,128]{3,2,1,0:T(8,128)(2,1)}, u32[]{:S(2)}) copy-start(bf16[1,16,128,128]{3,2,1,0:T(8,128)(2,1)} %param.10) | copy-start | bytes 1572868
  59.6 18.6 %copy-start.6 = (f32[128]{0:T(128)S(1)}, f32[128]{0:T(128)}, u32[]{:S(2)}) copy-start(f32[128]{0:T(128)} %param.18) | copy-start | bytes 1540
  60.8 9.1 %collective-permute-start.4 = (bf16[3,128,128]{2,1,0:T(8,128)(2,1)S(1)}, bf16[3,128,128]{2,1,0:T(8,128)(2,1)S(1)}, u32[]{:S(2)}, u32[]{:S(2)}) collective-permute-start(bf16[3,128,128]{2,1,0:T(8,128)(2,1)S(1)} %get-tuple-element.70), channel_id=1, source_target_pairs={{0,8},{8,16},{16,24},{24,32},{32,40},{40,48},{48,56},{56,64},{64,7... | collective-permute-start | bytes 294920 | tf_op jit(solution)/shard_map/ppermute | solution.py:20
  66.4 5.9 %collective-permute-start.5 = (bf16[3,128,128]{2,1,0:T(8,128)(2,1)S(1)}, bf16[3,128,128]{2,1,0:T(8,128)(2,1)S(1)}, u32[]{:S(2)}, u32[]{:S(2)}) collective-permute-start(bf16[3,128,128]{2,1,0:T(8,128)(2,1)S(1)} %get-tuple-element.71), channel_id=1, source_target_pairs={{8,0},{16,8},{24,16},{32,24},{40,32},{48,40},{56,48},{64,56},{72,6... | collective-permute-start | bytes 294920 | tf_op jit(solution)/shard_map/ppermute | solution.py:21
  69.8 97.6 %copy-start.3 = (bf16[1,16,128,128]{3,2,1,0:T(8,128)(2,1)S(1)}, bf16[1,16,128,128]{3,2,1,0:T(8,128)(2,1)}, u32[]{:S(2)}) copy-start(bf16[1,16,128,128]{3,2,1,0:T(8,128)(2,1)} %param.19) | copy-start | bytes 1572868
  72.4 94.9 %collective-permute-start.6 = (bf16[22,3,128]{2,1,0:T(4,128)(2,1)S(1)}, bf16[22,3,128]{2,1,0:T(4,128)(2,1)S(1)}, u32[]{:S(2)}, u32[]{:S(2)}) collective-permute-start(bf16[22,3,128]{2,1,0:T(4,128)(2,1)S(1)} %get-tuple-element.66), channel_id=1, source_target_pairs={{0,1},{1,2},{2,3},{3,4},{4,5},{5,6},{6,7},{8,9},{9,10},{10,11},{11... | collective-permute-start | bytes 50696 | tf_op jit(solution)/shard_map/ppermute | solution.py:20
  76.7 90.6 %collective-permute-start.7 = (bf16[22,3,128]{2,1,0:T(4,128)(2,1)S(1)}, bf16[22,3,128]{2,1,0:T(4,128)(2,1)S(1)}, u32[]{:S(2)}, u32[]{:S(2)}) collective-permute-start(bf16[22,3,128]{2,1,0:T(4,128)(2,1)S(1)} %get-tuple-element.67), channel_id=1, source_target_pairs={{1,0},{2,1},{3,2},{4,3},{5,4},{6,5},{7,6},{9,8},{10,9},{11,10},{12... | collective-permute-start | bytes 50696 | tf_op jit(solution)/shard_map/ppermute | solution.py:21
Sparse Core Ops, SparseCore 0:
  70.0 257.0 all-reduce.3
where the time goes:
time: 338 us; the launch traced here: 337 us
  waiting for transfers between devices  154 us (46%)
  blocking collectives  97.6 us (29%)
  other arithmetic  28.1 us (8%)
  starting transfers between devices  24.4 us (7%)
  between operations  14.4 us (4%)
  matrix products  11.4 us (3%)
  local copies, waits for them, and re-layouts  7.18 us (2%)
    psum x1, waiting for transfers between devices, on_device(): lax.psum((term_in, term_out, bias_term, kernel_term, gain_product), ('fsd...  151 us
    psum x1, blocking collectives, on_device(): lax.psum((term_in, term_out, bias_term, kernel_term, gain_product), ('fsd...  85.8 us
    ppermute x4, starting transfers between devices, padded_2(): before = lax.ppermute(last, axis, up)  17.8 us
    reduce_sum x1, other arithmetic, on_device(): center = jnp.mean(conv, axis=-1, keepdims=True)  8.22 us
    broadcast_in_dim x1, other arithmetic, on_device(): d_image[None]  8.14 us
    reduce_sum x3, other arithmetic, on_device(): jnp.sum(padded_f[row_tap:row_tap + height, col_tap:col_tap + width] * con...  7.12 us
  transfers between devices with their start and end apart: 9, of which 2 were waited for; matrix products, arithmetic and copies ran while one was open for 5% of the time, Pallas kernels for 0%

commit v1 on v0

v1 whole, which is shorter than its diff:
```python
import functools
import math

import jax
import jax.numpy as jnp
from jax import lax
from jax.experimental import pallas as pl
from jax.experimental.pallas import tpu as pltpu
from jax.sharding import PartitionSpec as P

MESH = pl.DeviceIdType.MESH
F32 = jnp.float32
BF16 = jnp.bfloat16

norm_eps = 1e-06
gelu_coef = math.sqrt(2.0 / math.pi)
cubic_coef = 0.044715

RH = 16
CW = 128
C = 128
HID = 512
XY = 16
NR = 16
NC = 8
BLOCK = 256
NBLOCKS = RH * CW // BLOCK

NT = (((1,), (1,)), ((), ()))
TN = (((0,), (0,)), ((), ()))


def tap_sums(source, first, rows, taps, acc, kb, flip):
    for b in range(7):
        weights = [kb[(6 - a) * 8 + (6 - b) if flip else a * 8 + b] for a in range(7)]
        for row in rows:
            value = source[row, pl.ds(first + 5 + b, 8), :]
            for h, a in taps(row):
                acc[h] = acc[h] + value * weights[a]
    return acc


def taps_all(row):
    return [(row - a, a) for a in range(7) if 0 <= row - a < RH]


def kernel(
    image, dw_kernel, dw_bias, gain, bias, w_in, b_in, w_out, b_out, cotangent,
    mixed_out, d_image_out, g_in_out, g_out_out, g_b_out, g_k_out, g_gain_out,
    img, cot, xp, dp, cv, kb, win, wout, mixed, dcb, dimg,
    gwi, gwo, bacc, gacc, kacc,
    hx_row, hx_col, hx_cor, hd_row, hd_col, hd_cor,
    grads, r1, small, r1s, s2, r2, a4, sa,
    local_sem, w_send, w_recv, hx_send, hx_recv, hd_send, hd_recv,
    s1_send, s1_recv, s1s_send, s1s_recv, s2_send, s2_recv, s3_send, s3_recv, s4_send, s4_recv, s4s_send, s4s_recv,
):
    mf = lax.axis_index("fsdp")
    mr = lax.axis_index("rows")
    mc = lax.axis_index("cols")
    me = mf * NC + mc

    def xy_id(peer):
        return (peer // NC, mr, peer % NC)

    def row_id(peer):
        return (mf, peer, mc)

    up, down = (mr + NR - 1) % NR, (mr + 1) % NR
    left, right = (mc + NC - 1) % NC, (mc + 1) % NC

    load_image = pltpu.make_async_copy(image, img, local_sem.at[0])
    load_image.start()
    load_cot = pltpu.make_async_copy(cotangent, cot, local_sem.at[1])
    load_cot.start()
    load_in = pltpu.make_async_copy(w_in, win.at[pl.ds(mf * 64, 64)], local_sem.at[2])
    load_in.start()
    load_out = pltpu.make_async_copy(w_out, wout.at[pl.ds(mf * 256, 256)], local_sem.at[3])
    load_out.start()

    barrier = pltpu.get_barrier_semaphore()

    def greet_xy(k, _):
        pl.semaphore_signal(barrier, inc=1, device_id=xy_id((me + k) % XY), device_id_type=MESH)
        return 0

    def greet_rows(k, _):
        pl.semaphore_signal(barrier, inc=1, device_id=row_id((mr + k) % NR), device_id_type=MESH)
        return 0

    corners = ((up, left), (up, right), (down, left), (down, right))
    for r, c in corners:
        pl.semaphore_signal(barrier, inc=1, device_id=(mf, r, c), device_id_type=MESH)
    lax.fori_loop(1, XY, greet_xy, 0)
    lax.fori_loop(1, NR, greet_rows, 0)
    pl.semaphore_wait(barrier, 4 + XY - 1 + NR - 1)

    def halo(source, rows_buf, col_buf, cor_buf, send, recv):
        plan = [
            (source.at[pl.ds(RH - 3, 3)], rows_buf.at[0], (mf, down, mc)),
            (source.at[pl.ds(0, 3)], rows_buf.at[1], (mf, up, mc)),
            (source.at[:, pl.ds(CW - 16, 16)], col_buf.at[0], (mf, mr, right)),
            (source.at[:, pl.ds(0, 16)], col_buf.at[1], (mf, mr, left)),
            (source.at[pl.ds(RH - 3, 3), pl.ds(CW - 16, 16)], cor_buf.at[0], (mf, down, right)),
            (source.at[pl.ds(RH - 3, 3), pl.ds(0, 16)], cor_buf.at[1], (mf, down, left)),
            (source.at[pl.ds(0, 3), pl.ds(CW - 16, 16)], cor_buf.at[2], (mf, up, right)),
            (source.at[pl.ds(0, 3), pl.ds(0, 16)], cor_buf.at[3], (mf, up, left)),
        ]
        copies = []
        for i, (src, dst, target) in enumerate(plan):
            copy = pltpu.make_async_remote_copy(
                src_ref=src, dst_ref=dst, send_sem=send.at[i], recv_sem=recv.at[i], device_id=target, device_id_type=MESH
            )
            copy.start()
            copies.append(copy)
        return copies

    has_up = jnp.where(mr > 0, 1.0, 0.0).astype(F32)
    has_down = jnp.where(mr < NR - 1, 1.0, 0.0).astype(F32)
    has_left = jnp.where(mc > 0, 1.0, 0.0).astype(F32)
    has_right = jnp.where(mc < NC - 1, 1.0, 0.0).astype(F32)

    def unpack_halo(padded, rows_buf, col_buf, cor_buf):
        for i in range(3):
            padded[i, pl.ds(8, CW), :] = rows_buf[0, i].astype(F32) * has_up
            padded[RH + 3 + i, pl.ds(8, CW), :] = rows_buf[1, i].astype(F32) * has_down
            padded[i, pl.ds(0, 8), :] = cor_buf[0, i].astype(F32)[8:16] * (has_up * has_left)
            padded[i, pl.ds(CW + 8, 8), :] = cor_buf[1, i].astype(F32)[0:8] * (has_up * has_right)
            padded[RH + 3 + i, pl.ds(0, 8), :] = cor_buf[2, i].astype(F32)[8:16] * (has_down * has_left)
            padded[RH + 3 + i, pl.ds(CW + 8, 8), :] = cor_buf[3, i].astype(F32)[0:8] * (has_down * has_right)

        def side(r, _):
            padded[3 + r, pl.ds(0, 8), :] = col_buf[0, r].astype(F32)[8:16] * has_left
            padded[3 + r, pl.ds(CW + 8, 8), :] = col_buf[1, r].astype(F32)[0:8] * has_right
            return 0

        lax.fori_loop(0, RH, side, 0)

    hx = halo(image, hx_row, hx_col, hx_cor, hx_send, hx_recv)
    partner = (1 - mf, mr, mc)
    send_in = pltpu.make_async_remote_copy(
        src_ref=w_in, dst_ref=win.at[pl.ds(mf * 64, 64)], send_sem=w_send.at[0], recv_sem=w_recv.at[0],
        device_id=partner, device_id_type=MESH,
    )
    send_in.start()
    send_out = pltpu.make_async_remote_copy(
        src_ref=w_out, dst_ref=wout.at[pl.ds(mf * 256, 256)], send_sem=w_send.at[1], recv_sem=w_recv.at[1],
        device_id=partner, device_id_type=MESH,
    )
    send_out.start()

    for a in range(7):
        for b in range(7):
            kb[a * 8 + b] = jnp.broadcast_to(dw_kernel[a, pl.ds(b, 1), :], (8, C))
    conv_bias = jnp.broadcast_to(dw_bias[...], (8, C))

    load_image.wait()

    def widen(r, _):
        xp[3 + r, pl.ds(8, CW), :] = img[r].astype(F32)
        return 0

    lax.fori_loop(0, RH, widen, 0)

    own_rows = range(3, RH + 3)
    edge_rows = (0, 1, 2, RH + 3, RH + 4, RH + 5)

    def conv_inner(wb, _):
        first = pl.multiple_of(wb * 8, 8)
        acc = tap_sums(xp, first, own_rows, taps_all, [conv_bias] * RH, kb, False)
        for h in range(RH):
            cv[h, pl.ds(first, 8), :] = acc[h]
        return 0

    lax.fori_loop(1, CW // 8 - 1, conv_inner, 0)

    for copy in hx:
        copy.wait_recv()
    unpack_halo(xp, hx_row, hx_col, hx_cor)

    def conv_edge(wb, _):
        first = pl.multiple_of(wb * 8, 8)
        acc = [None] * RH
        touched = (0, 1, 2, RH - 3, RH - 2, RH - 1)
        for h in touched:
            acc[h] = cv[h, pl.ds(first, 8), :]
        acc = tap_sums(xp, first, edge_rows, taps_all, acc, kb, False)
        for h in touched:
            cv[h, pl.ds(first, 8), :] = acc[h]
        return 0

    lax.fori_loop(1, CW // 8 - 1, conv_edge, 0)

    def conv_side(i, _):
        first = pl.multiple_of(i * (CW - 8), 8)
        acc = tap_sums(xp, first, range(RH + 6), taps_all, [conv_bias] * RH, kb, False)
        for h in range(RH):
            cv[h, pl.ds(first, 8), :] = acc[h]
        return 0

    lax.fori_loop(0, 2, conv_side, 0)

    load_in.wait()
    load_out.wait()
    load_cot.wait()
    send_in.wait_recv()
    send_out.wait_recv()
    gwi[...] = jnp.zeros_like(gwi)
    gwo[...] = jnp.zeros_like(gwo)
    bacc[...] = jnp.zeros_like(bacc)
    gacc[...] = jnp.zeros_like(gacc)
    rows_per = BLOCK // CW

    def pointwise(i, _):
        r0 = i * rows_per
        conv = cv[pl.ds(r0, rows_per)].reshape(BLOCK, C)
        center = jnp.mean(conv, axis=-1, keepdims=True)
        spread = conv - center
        rstd = lax.rsqrt(jnp.mean(spread * spread, axis=-1, keepdims=True) + norm_eps)
        xhat = spread * rstd
        normed = (xhat * gain[...] + bias[...]).astype(BF16)
        up_b = cot[pl.ds(r0, rows_per)].reshape(BLOCK, C)
        out_sum = jnp.zeros((BLOCK, C), F32)
        dn = jnp.zeros((BLOCK, C), F32)
        half = HID // 2
        for j in range(2):
            cols = slice(j * half, (j + 1) * half)
            pre = jnp.dot(normed, win[:, cols], preferred_element_type=F32) + b_in[:, cols]
            square = pre * pre
            tanh_val = jnp.tanh(pre * (gelu_coef + (gelu_coef * cubic_coef) * square))
            half_gate = 0.5 + 0.5 * tanh_val
            hidden = (pre * half_gate).astype(BF16)
            slope = half_gate + (pre * (0.5 - 0.5 * tanh_val * tanh_val)) * (
                gelu_coef + (3.0 * gelu_coef * cubic_coef) * square
            )
            d_hidden = lax.dot_general(up_b, wout[cols, :], NT, preferred_element_type=F32)
            d_wide = d_hidden * slope
            d_pre = d_wide.astype(BF16)
            bacc[:, cols] += jnp.sum(d_wide.reshape(BLOCK // 8, 8, half), axis=0)
            out_sum = out_sum + jnp.dot(hidden, wout[cols, :], preferred_element_type=F32)
            dn = dn + lax.dot_general(d_pre, win[:, cols], NT, preferred_element_type=F32)
            gwi[:, cols] += lax.dot_general(normed, d_pre, TN, preferred_element_type=F32)
            gwo[:, cols] += lax.dot_general(up_b, hidden, TN, preferred_element_type=F32)
        field = img[pl.ds(r0, rows_per)].reshape(BLOCK, C).astype(F32)
        mixed[pl.ds(r0, rows_per)] = (field + out_sum + b_out[...]).astype(BF16).reshape(rows_per, CW, C)
        gacc[...] += jnp.sum((dn * xhat).reshape(BLOCK // 8, 8, C), axis=0)
        q = dn * gain[...]
        d_conv = (
            rstd * (q - jnp.mean(q, axis=-1, keepdims=True) - xhat * jnp.mean(q * xhat, axis=-1, keepdims=True))
        ).astype(BF16)
        d_rows = d_conv.reshape(rows_per, CW, C)
        dcb[pl.ds(r0, rows_per)] = d_rows
        dp[pl.ds(3 + r0, rows_per), pl.ds(8, CW), :] = d_rows.astype(F32)
        return 0

    lax.fori_loop(0, NBLOCKS, pointwise, 0)

    hd = halo(dcb, hd_row, hd_col, hd_cor, hd_send, hd_recv)
    save_mixed = pltpu.make_async_copy(mixed, mixed_out, local_sem.at[4])
    save_mixed.start()

    for q in range(4):
        turned = gwo[:, q * 128 : (q + 1) * 128].T
        for u in range(16):
            tile = turned[u * 8 : (u + 1) * 8]
            at = q * 4 + u // 4
            grads[at, 8 + 2 * (u % 4)] = tile[0:4]
            grads[at, 9 + 2 * (u % 4)] = tile[4:8]

    def deal(p, _):
        rows = gwi[pl.ds(pl.multiple_of(p * 8, 8), 8), :]
        for q in range(4):
            tile = rows[:, q * 128 : (q + 1) * 128]
            grads[p, 2 * q] = tile[0:4]
            grads[p, 2 * q + 1] = tile[4:8]
        return 0

    lax.fori_loop(0, XY, deal, 0)

    def copy_1(k):
        peer = (me + k) % XY
        return pltpu.make_async_remote_copy(
            src_ref=grads.at[peer], dst_ref=r1.at[k], send_sem=s1_send.at[k], recv_sem=s1_recv.at[k],
            device_id=xy_id(peer), device_id_type=MESH,
        )

    def copy_1s(k):
        peer = (me + k) % XY
        return pltpu.make_async_remote_copy(
            src_ref=small.at[peer], dst_ref=r1s.at[k], send_sem=s1s_send.at[k], recv_sem=s1s_recv.at[k],
            device_id=xy_id(peer), device_id_type=MESH,
        )

    def copy_2(k):
        peer = (mr + k) % NR
        return pltpu.make_async_remote_copy(
            src_ref=s2.at[peer], dst_ref=r2.at[mr], send_sem=s2_send.at[k], recv_sem=s2_recv.at[k],
            device_id=row_id(peer), device_id_type=MESH,
        )

    def copy_3(k):
        peer = (mr + k) % NR
        return pltpu.make_async_remote_copy(
            src_ref=a4.at[mc, mr], dst_ref=a4.at[mc, mr], send_sem=s3_send.at[k], recv_sem=s3_recv.at[k],
            device_id=row_id(peer), device_id_type=MESH,
        )

    def copy_4(k):
        return pltpu.make_async_remote_copy(
            src_ref=a4.at[mc], dst_ref=a4.at[mc], send_sem=s4_send.at[k], recv_sem=s4_recv.at[k],
            device_id=(mf, mr, (mc + k) % NC), device_id_type=MESH,
        )

    def copy_4s(k):
        return pltpu.make_async_remote_copy(
            src_ref=sa.at[me], dst_ref=sa.at[me], send_sem=s4s_send.at[k], recv_sem=s4s_recv.at[k],
            device_id=xy_id((me + k) % XY), device_id_type=MESH,
        )

    def each(count, act):
        def step(k, _):
            act(k)
            return 0

        lax.fori_loop(1, count, step, 0)

    each(XY, lambda k: copy_1(k).start())

    def tap_gradient(b):
        def step(wb, acc):
            first = pl.multiple_of(wb * 8, 8)
            acc = list(acc)
            grad = [dp[3 + h, pl.ds(first + 8, 8), :] for h in range(RH)]
            for row in range(RH + 6):
                value = xp[row, pl.ds(first + 5 + b, 8), :]
                for h, a in taps_all(row):
                    acc[a] = acc[a] + value * grad[h]
            return tuple(acc)

        acc = lax.fori_loop(0, CW // 8, step, tuple(jnp.zeros((8, C), F32) for _ in range(7)))
        for a in range(7):
            kacc[pl.ds((a * 8 + b) * 8, 8), :] = acc[a]

    for b in range(7):
        tap_gradient(b)
    for a in range(7):
        kacc[pl.ds((a * 8 + 7) * 8, 8), :] = jnp.zeros((8, C), F32)
    for a in range(7):
        total = kacc[pl.ds(a * 64, 8, stride=8), :]
        for s in range(1, 8):
            total = total + kacc[pl.ds(a * 64 + s, 8, stride=8), :]
        small[2 * a] = total[0:4]
        small[2 * a + 1] = total[4:8]
    for q in range(4):
        small[14, pl.ds(q, 1), :] = jnp.sum(bacc[:, q * 128 : (q + 1) * 128], axis=0, keepdims=True)
    small[15] = jnp.broadcast_to(jnp.sum(gacc[...], axis=0, keepdims=True), (4, C))
    each(XY, lambda k: copy_1s(k).start())

    for copy in hd:
        copy.wait_recv()
    unpack_halo(dp, hd_row, hd_col, hd_cor)

    def image_gradient(wb, _):
        first = pl.multiple_of(wb * 8, 8)
        acc = tap_sums(dp, first, range(RH + 6), taps_all, [jnp.zeros((8, C), F32)] * RH, kb, True)
        for h in range(RH):
            cv[h, pl.ds(first, 8), :] = acc[h]
        return 0

    lax.fori_loop(0, 8, image_gradient, 0)

    each(XY, lambda k: copy_1(k).wait_recv())
    each(XY, lambda k: copy_1s(k).wait_recv())
    little = small[me]
    for k in range(1, XY):
        little = little + r1s[k]

    def sum_1(r, _):
        total = grads[me, r]
        for k in range(1, XY):
            total = total + r1[k, r]
        s2[r, 0] = total
        s2[r, 1] = little
        return 0

    lax.fori_loop(0, NR, sum_1, 0)
    each(NR, lambda k: copy_2(k).start())
    r2[mr] = s2[mr]

    lax.fori_loop(8, 12, image_gradient, 0)

    each(NR, lambda k: copy_2(k).wait_recv())
    total = r2[0]
    for s in range(1, NR):
        total = total + r2[s]
    a4[mc, mr] = total[0]
    sa[me] = total[1]
    each(NR, lambda k: copy_3(k).start())
    each(XY, lambda k: copy_4s(k).start())

    lax.fori_loop(12, 16, image_gradient, 0)

    each(NR, lambda k: copy_3(k).wait_recv())
    each(NC, lambda k: copy_4(k).start())

    def finish(r, _):
        dimg[r] = (cot[r].astype(F32) + cv[r]).astype(BF16)
        return 0

    lax.fori_loop(0, RH, finish, 0)
    save_grad = pltpu.make_async_copy(dimg, d_image_out, local_sem.at[5])
    save_grad.start()

    each(XY, lambda k: copy_4s(k).wait_recv())
    for a in range(7):
        g_k_out[a, pl.ds(0, 4), :] = sa[2 * a]
        g_k_out[a, pl.ds(4, 3), :] = sa[2 * a + 1][0:3]
    for q in range(4):
        g_b_out[:, q * 128 : (q + 1) * 128] = sa[14, pl.ds(q, 1), :]
    g_gain_out[...] = sa[15, pl.ds(0, 1), :]

    each(NC, lambda k: copy_4(k).wait_recv())

    def place(j, _):
        for q in range(4):
            at = pl.multiple_of(j * 8, 8)
            g_in_out[pl.ds(at, 8), q * 128 : (q + 1) * 128] = jnp.concatenate([a4[j, 2 * q], a4[j, 2 * q + 1]], axis=0)
            at = pl.multiple_of(j * 32 + q * 8, 8)
            g_out_out[pl.ds(at, 8), :] = jnp.concatenate([a4[j, 8 + 2 * q], a4[j, 9 + 2 * q]], axis=0)
        return 0

    lax.fori_loop(0, NC, place, 0)

    for copy in hx:
        copy.wait_send()
    for copy in hd:
        copy.wait_send()
    send_in.wait_send()
    send_out.wait_send()
    each(XY, lambda k: copy_1(k).wait_send())
    each(XY, lambda k: copy_1s(k).wait_send())
    each(NR, lambda k: copy_2(k).wait_send())
    each(NR, lambda k: copy_3(k).wait_send())
    each(XY, lambda k: copy_4s(k).wait_send())
    each(NC, lambda k: copy_4(k).wait_send())
    save_mixed.wait()
    save_grad.wait()


def on_device(
    image, dw_kernel, dw_bias, layer_norm_gain, layer_norm_bias, w_in, b_in, w_out, b_out, cotangent
):
    vmem = pl.BlockSpec(memory_space=pltpu.VMEM)
    hbm = pl.BlockSpec(memory_space=pl.ANY)
    sem = pltpu.SemaphoreType.DMA
    scratch = [
        pltpu.VMEM((RH, CW, C), BF16),
        pltpu.VMEM((RH, CW, C), BF16),
        pltpu.VMEM((RH + 6, CW + 16, C), F32),
        pltpu.VMEM((RH + 6, CW + 16, C), F32),
        pltpu.VMEM((RH, CW, C), F32),
        pltpu.VMEM((56, 8, C), F32),
        pltpu.VMEM((C, HID), BF16),
        pltpu.VMEM((HID, C), BF16),
        pltpu.VMEM((RH, CW, C), BF16),
        pltpu.VMEM((RH, CW, C), BF16),
        pltpu.VMEM((RH, CW, C), BF16),
        pltpu.VMEM((C, HID), F32),
        pltpu.VMEM((C, HID), F32),
        pltpu.VMEM((8, HID), F32),
        pltpu.VMEM((8, C), F32),
        pltpu.VMEM((448, C), F32),
    ]
    for _ in range(2):
        scratch += [
            pltpu.VMEM((2, 3, CW, C), BF16),
            pltpu.VMEM((2, RH, 16, C), BF16),
            pltpu.VMEM((4, 3, 16, C), BF16),
        ]
    scratch += [
        pltpu.VMEM((XY, NR, 4, C), F32),
        pltpu.VMEM((XY, NR, 4, C), F32),
        pltpu.VMEM((XY, 4, C), F32),
        pltpu.VMEM((XY, 4, C), F32),
        pltpu.VMEM((NR, 2, 4, C), F32),
        pltpu.VMEM((NR, 2, 4, C), F32),
        pltpu.VMEM((NC, NR, 4, C), F32),
        pltpu.VMEM((XY, 4, C), F32),
        sem((6,)), sem((2,)), sem((2,)), sem((8,)), sem((8,)), sem((8,)), sem((8,)),
    ] + [sem((16,)) for _ in range(12)]
    outs = pl.pallas_call(
        kernel,
        out_shape=(
            jax.ShapeDtypeStruct((RH, CW, C), BF16),
            jax.ShapeDtypeStruct((RH, CW, C), BF16),
            jax.ShapeDtypeStruct((C // 2, HID), F32),
            jax.ShapeDtypeStruct((HID // 2, C), F32),
            jax.ShapeDtypeStruct((1, HID), F32),
            jax.ShapeDtypeStruct((7, 7, C), F32),
            jax.ShapeDtypeStruct((1, C), F32),
        ),
        in_specs=[hbm, vmem, vmem, vmem, vmem, hbm, vmem, hbm, vmem, hbm],
        out_specs=(hbm, hbm, vmem, vmem, vmem, vmem, vmem),
        scratch_shapes=scratch,
        compiler_params=pltpu.CompilerParams(
            collective_id=0, has_side_effects=True, vmem_limit_bytes=48 * 1024 * 1024
        ),
        name="convnext_block",
    )(
        image[0], dw_kernel, dw_bias.reshape(1, C), layer_norm_gain.reshape(1, C), layer_norm_bias.reshape(1, C),
        w_in, b_in.reshape(1, HID), w_out, b_out.reshape(1, C), cotangent[0],
    )
    mixed, d_image, g_in, g_out, g_b, g_k, g_gain = outs
    return (mixed[None], d_image[None], g_in, g_out, g_b.reshape(HID), g_k, g_gain.reshape(C))


def solution(mesh):
    return jax.shard_map(
        on_device,
        mesh=mesh,
        in_specs=(
            P("fsdp", "rows", "cols", None),
            P(),
            P(),
            P(),
            P(),
            P("fsdp", None),
            P(),
            P("fsdp", None),
            P(),
            P("fsdp", "rows", "cols", None),
        ),
        out_specs=(
            P("fsdp", "rows", "cols", None),
            P("fsdp", "rows", "cols", None),
            P("fsdp", None),
            P("fsdp", None),
            P(),
            P(),
            P(),
        ),
        check_vma=False,
    )
```

time: 338 us -> 67.6 us (0.20)
  waiting for transfers between devices: 154 us -> 0 us
  blocking collectives: 97.6 us -> 0 us
  Pallas kernels: 0 us -> 56.7 us
  other arithmetic: 28.1 us -> 0 us
  starting transfers between devices: 24.4 us -> 0 us
  between operations: 14.4 us -> 0.69 us
  matrix products: 11.4 us -> 0 us
    psum x1 -> x0, waiting for transfers between devices: 151 us -> none  [on_device(): lax.psum((term_in, term_out, bias_term, kernel_term, gain_product), ('fsd...]
    psum x1 -> x0, blocking collectives: 85.8 us -> none  [on_device(): lax.psum((term_in, term_out, bias_term, kernel_term, gain_product), ('fsd...]
    pallas_call x0 -> x1, Pallas kernels: none -> 56.7 us  [on_device(): pl.pallas_call(kernel, out_shape=(jax.ShapeDtypeStruct((RH, CW, C), BF16)...]
    ppermute x8 -> x0, starting transfers between devices: 24.4 us -> none  [the longest x4 17.8 us: padded_2(): before = lax.ppermute(last, axis, up)]
    reduce_sum x6 -> x0, other arithmetic: 17 us -> none  [the longest x1 8.22 us: on_device(): center = jnp.mean(conv, axis=-1, keepdims=True)]
    all_gather x2 -> x0, blocking collectives: 11.8 us -> none  [the longest x1 6.14 us: on_device(): lax.all_gather(w_out, 'fsdp', axis=0, tiled=True)]
    dot_general x6 -> x0, matrix products: 11.4 us -> none  [the longest x1 3.13 us: on_device(): lax.dot_general(flat_up, full_out, contract_cols, preferred_element_type=...]
    unnamed x16 -> x27, local copies, waits for them, and re-layouts: 0.05 us -> 9.78 us
  transfers between devices with their start and end apart: 9 -> 0, of which waited for: 2 -> 0; matrix products, arithmetic and copies ran while one was open for 5% -> 0% of each run, Pallas kernels for 0% -> 0%
where the time goes in v1:
time: 67.6 us; the launch traced here: 67.2 us
  Pallas kernels  56.7 us (84%)
  local copies, waits for them, and re-layouts  9.78 us (14%)
  between operations  0.69 us (1%)
    pallas_call x1, Pallas kernels, on_device(): pl.pallas_call(kernel, out_shape=(jax.ShapeDtypeStruct((RH, CW, C), BF16)...  56.7 us
    unnamed x27, local copies, waits for them, and re-layouts  9.78 us

profile of v1, /device:TPU:1, one launch (start us, length us, event | category | flops | bytes accessed | tf_op | source)
XLA Modules:
  0.0 67.2 jit_solution(3646379224936532636)
XLA Ops:
  0.6 0.0 copy-start.9
  0.6 0.0 copy-start.5
  0.7 0.0 copy-start.6
  0.7 0.0 copy-start.7
  0.7 0.0 copy-start.8
  0.7 0.6 copy-done.9
  1.3 0.0 copy-done.5
  1.3 0.0 copy-done.6
  1.3 0.0 copy-done.7
  1.3 0.0 copy-done.8
  1.4 0.0 copy-start
  1.4 1.0 %copy-done = bf16[1,16,128,128]{3,2,1,0:T(8,128)(2,1)S(1)} copy-done((bf16[1,16,128,128]{3,2,1,0:T(8,128)(2,1)S(1)}, bf16[1,16,128,128]{3,2,1,0:T(8,128)(2,1)}, u32[]{:S(2)}) %copy-start) | copy-done | bytes 524312
  2.4 0.0 copy-start.1
  2.4 1.0 %copy-done.1 = bf16[1,16,128,128]{3,2,1,0:T(8,128)(2,1)S(1)} copy-done((bf16[1,16,128,128]{3,2,1,0:T(8,128)(2,1)S(1)}, bf16[1,16,128,128]{3,2,1,0:T(8,128)(2,1)}, u32[]{:S(2)}) %copy-start.1) | copy-done | bytes 524312
  3.4 0.0 copy-start.2
  3.4 0.8 %copy-done.2 = bf16[64,512]{1,0:T(8,128)(2,1)S(1)} copy-done((bf16[64,512]{1,0:T(8,128)(2,1)S(1)}, bf16[64,512]{1,0:T(8,128)(2,1)}, u32[]{:S(2)}) %copy-start.2) | copy-done | bytes 65560
  4.3 0.0 copy-start.3
  4.3 0.8 %copy-done.3 = bf16[256,128]{1,0:T(8,128)(2,1)S(1)} copy-done((bf16[256,128]{1,0:T(8,128)(2,1)S(1)}, bf16[256,128]{1,0:T(8,128)(2,1)}, u32[]{:S(2)}) %copy-start.3) | copy-done | bytes 65560
  5.1 0.0 copy-start.4
  5.1 0.7 %copy-done.4 = f32[7,7,128]{2,1,0:T(8,128)S(1)} copy-done((f32[7,7,128]{2,1,0:T(8,128)S(1)}, f32[7,7,128]{2,1,0:T(8,128)}, u32[]{:S(2)}) %copy-start.4) | copy-done | bytes 25112
  5.9 56.7 %convnext_block.1 = (bf16[16,128,128]{2,1,0:T(8,128)(2,1)S(1)}, bf16[16,128,128]{2,1,0:T(8,128)(2,1)S(1)}, f32[64,512]{1,0:T(8,128)S(1)}, f32[256,128]{1,0:T(8,1...) custom-call(bf16[16,128,128]{2,1,0:T(8,128)(2,1)S(1)} %bitcast.11, ...), custom_call_target="tpu_custom_call" | custom-call | tf_op jit(solution)/shard_map/convnext_block/pallas_call | solution.py:490
  62.6 0.8 %copy.24 = bf16[1,16,128,128]{3,2,1,0:T(8,128)(2,1)} copy(bf16[1,16,128,128]{3,2,1,0:T(8,128)(2,1)S(1)} %bitcast.14) | data formatting | bytes 1048576
  63.4 0.8 %copy.25 = bf16[1,16,128,128]{3,2,1,0:T(8,128)(2,1)} copy(bf16[1,16,128,128]{3,2,1,0:T(8,128)(2,1)S(1)} %bitcast.13) | data formatting | bytes 1048576
  64.2 0.7 copy.26
  64.9 0.7 copy.27
  65.5 0.6 copy.28
  66.1 0.6 copy.29
  66.7 0.5 copy.30
Async XLA Ops:
  0.6 0.7 copy-start.9
  0.6 0.7 %copy-start.5 = (f32[512]{0:T(512)S(1)}, f32[512]{0:T(512)}, u32[]{:S(2)}) copy-start(f32[512]{0:T(512)} %param.16) | copy-start | bytes 6148
  0.7 0.7 %copy-start.6 = (f32[128]{0:T(128)S(1)}, f32[128]{0:T(128)}, u32[]{:S(2)}) copy-start(f32[128]{0:T(128)} %param.12) | copy-start | bytes 1540
  0.7 0.7 %copy-start.7 = (f32[128]{0:T(128)S(1)}, f32[128]{0:T(128)}, u32[]{:S(2)}) copy-start(f32[128]{0:T(128)} %param.13) | copy-start | bytes 1540
  0.7 0.7 %copy-start.8 = (f32[128]{0:T(128)S(1)}, f32[128]{0:T(128)}, u32[]{:S(2)}) copy-start(f32[128]{0:T(128)} %param.14) | copy-start | bytes 1540
  1.4 1.0 %copy-start = (bf16[1,16,128,128]{3,2,1,0:T(8,128)(2,1)S(1)}, bf16[1,16,128,128]{3,2,1,0:T(8,128)(2,1)}, u32[]{:S(2)}) copy-start(bf16[1,16,128,128]{3,2,1,0:T(8,128)(2,1)} %param.10) | copy-start | bytes 1572868
  2.4 1.0 %copy-start.1 = (bf16[1,16,128,128]{3,2,1,0:T(8,128)(2,1)S(1)}, bf16[1,16,128,128]{3,2,1,0:T(8,128)(2,1)}, u32[]{:S(2)}) copy-start(bf16[1,16,128,128]{3,2,1,0:T(8,128)(2,1)} %param.19) | copy-start | bytes 1572868
  3.4 0.8 %copy-start.2 = (bf16[64,512]{1,0:T(8,128)(2,1)S(1)}, bf16[64,512]{1,0:T(8,128)(2,1)}, u32[]{:S(2)}) copy-start(bf16[64,512]{1,0:T(8,128)(2,1)} %w_in.1) | copy-start | bytes 196612
  4.3 0.8 %copy-start.3 = (bf16[256,128]{1,0:T(8,128)(2,1)S(1)}, bf16[256,128]{1,0:T(8,128)(2,1)}, u32[]{:S(2)}) copy-start(bf16[256,128]{1,0:T(8,128)(2,1)} %w_out.1) | copy-start | bytes 196612
  5.1 0.7 %copy-start.4 = (f32[7,7,128]{2,1,0:T(8,128)S(1)}, f32[7,7,128]{2,1,0:T(8,128)}, u32[]{:S(2)}) copy-start(f32[7,7,128]{2,1,0:T(8,128)} %dw_kernel.1) | copy-start | bytes 75268

commit v2 on v1

--- a/solution.py
+++ b/solution.py
@@ -45,19 +45,21 @@
 
 
 def kernel(
-    image, dw_kernel, dw_bias, gain, bias, w_in, b_in, w_out, b_out, cotangent,
+    image, dw_kernel_in, dw_bias_in, gain_in, bias_in, w_in, b_in_in, w_out, b_out_in, cotangent,
     mixed_out, d_image_out, g_in_out, g_out_out, g_b_out, g_k_out, g_gain_out,
-    img, cot, xp, dp, cv, kb, win, wout, mixed, dcb, dimg,
+    mixed, dimg, g_out, g_b, g_k, g_gain, img, cot, dw_kernel, dw_bias, gain, bias, b_in, b_out, xp, dp, cv, kb, win, wout, dcb,
     gwi, gwo, bacc, gacc, kacc,
     hx_row, hx_col, hx_cor, hd_row, hd_col, hd_cor,
-    grads, r1, small, r1s, s2, r2, a4, sa,
-    local_sem, w_send, w_recv, hx_send, hx_recv, hd_send, hd_recv,
-    s1_send, s1_recv, s1s_send, s1s_recv, s2_send, s2_recv, s3_send, s3_recv, s4_send, s4_recv, s4s_send, s4s_recv,
+    grads, from_core, pair, r1, r2, a4, small, r1s, r2s, sa,
+    local_sem, w_send, w_recv, hx_send, hx_recv, hd_send, hd_recv, x_send, x_recv, out_sem,
 ):
     mf = lax.axis_index("fsdp")
     mr = lax.axis_index("rows")
     mc = lax.axis_index("cols")
     me = mf * NC + mc
+    core = mr % 2
+    other = mr + 1 - 2 * core
+    mz = mr // 2
 
     def xy_id(peer):
         return (peer // NC, mr, peer % NC)
@@ -68,31 +70,65 @@
     up, down = (mr + NR - 1) % NR, (mr + 1) % NR
     left, right = (mc + NC - 1) % NC, (mc + 1) % NC
 
-    load_image = pltpu.make_async_copy(image, img, local_sem.at[0])
-    load_image.start()
-    load_cot = pltpu.make_async_copy(cotangent, cot, local_sem.at[1])
-    load_cot.start()
-    load_in = pltpu.make_async_copy(w_in, win.at[pl.ds(mf * 64, 64)], local_sem.at[2])
-    load_in.start()
-    load_out = pltpu.make_async_copy(w_out, wout.at[pl.ds(mf * 256, 256)], local_sem.at[3])
-    load_out.start()
+    loads = [
+        (image, img), (cotangent, cot), (dw_kernel_in, dw_kernel), (dw_bias_in, dw_bias), (gain_in, gain), (bias_in, bias),
+        (b_in_in, b_in), (b_out_in, b_out), (w_in, win.at[pl.ds(mf * 64, 64)]), (w_out, wout.at[pl.ds(mf * 256, 256)]),
+    ]
+    loads = [pltpu.make_async_copy(src, dst, local_sem.at[i]) for i, (src, dst) in enumerate(loads)]
+    for i in (2, 3, 0, 1, 4, 5, 6, 7, 8, 9):
+        loads[i].start()
 
     barrier = pltpu.get_barrier_semaphore()
 
+    def greet(device):
+        pl.semaphore_signal(barrier, inc=1, device_id=device, device_id_type=MESH)
+
     def greet_xy(k, _):
-        pl.semaphore_signal(barrier, inc=1, device_id=xy_id((me + k) % XY), device_id_type=MESH)
+        greet(xy_id((me + k) % XY))
         return 0
 
     def greet_rows(k, _):
-        pl.semaphore_signal(barrier, inc=1, device_id=row_id((mr + k) % NR), device_id_type=MESH)
-        return 0
-
-    corners = ((up, left), (up, right), (down, left), (down, right))
-    for r, c in corners:
-        pl.semaphore_signal(barrier, inc=1, device_id=(mf, r, c), device_id_type=MESH)
+        greet(row_id((mr + k) % NR))
+        return 0
+
+    def greet_other(k, _):
+        greet((mf, other, (mc + k) % NC))
+        return 0
+
+    beyond = (mr + NR - 1 + 2 * core) % NR
+    greet((mf, beyond, left))
+    greet((mf, beyond, right))
+    lax.fori_loop(1, NC, greet_other, 0)
     lax.fori_loop(1, XY, greet_xy, 0)
     lax.fori_loop(1, NR, greet_rows, 0)
-    pl.semaphore_wait(barrier, 4 + XY - 1 + NR - 1)
+
+    loads[2].wait()
+    loads[3].wait()
+    for a in range(7):
+        for b in range(7):
+            kb[a * 8 + b] = jnp.broadcast_to(dw_kernel[a, pl.ds(b, 1), :], (8, C))
+    conv_bias = jnp.broadcast_to(dw_bias[...], (8, C))
+
+    loads[0].wait()
+
+    def widen(r, _):
+        xp[3 + r, pl.ds(8, CW), :] = img[r].astype(F32)
+        return 0
+
+    lax.fori_loop(0, RH, widen, 0)
+
+    own_rows = range(3, RH + 3)
+    edge_rows = (0, 1, 2, RH + 3, RH + 4, RH + 5)
+
+    def conv_inner(wb, _):
+        first = pl.multiple_of(wb * 8, 8)
+        acc = tap_sums(xp, first, own_rows, taps_all, [conv_bias] * RH, kb, False)
+        for h in range(RH):
+            cv[h, pl.ds(first, 8), :] = acc[h]
+        return 0
+
+    lax.fori_loop(1, 4, conv_inner, 0)
+    pl.semaphore_wait(barrier, 2 + NC - 1 + XY - 1 + NR - 1)
 
     def halo(source, rows_buf, col_buf, cor_buf, send, recv):
         plan = [
@@ -148,30 +184,7 @@
     )
     send_out.start()
 
-    for a in range(7):
-        for b in range(7):
-            kb[a * 8 + b] = jnp.broadcast_to(dw_kernel[a, pl.ds(b, 1), :], (8, C))
-    conv_bias = jnp.broadcast_to(dw_bias[...], (8, C))
-
-    load_image.wait()
-
-    def widen(r, _):
-        xp[3 + r, pl.ds(8, CW), :] = img[r].astype(F32)
-        return 0
-
-    lax.fori_loop(0, RH, widen, 0)
-
-    own_rows = range(3, RH + 3)
-    edge_rows = (0, 1, 2, RH + 3, RH + 4, RH + 5)
-
-    def conv_inner(wb, _):
-        first = pl.multiple_of(wb * 8, 8)
-        acc = tap_sums(xp, first, own_rows, taps_all, [conv_bias] * RH, kb, False)
-        for h in range(RH):
-            cv[h, pl.ds(first, 8), :] = acc[h]
-        return 0
-
-    lax.fori_loop(1, CW // 8 - 1, conv_inner, 0)
+    lax.fori_loop(4, CW // 8 - 1, conv_inner, 0)
 
     for copy in hx:
         copy.wait_recv()
@@ -199,9 +212,8 @@
 
     lax.fori_loop(0, 2, conv_side, 0)
 
-    load_in.wait()
-    load_out.wait()
-    load_cot.wait()
+    for i in (1, 4, 5, 6, 7, 8, 9):
+        loads[i].wait()
     send_in.wait_recv()
     send_out.wait_recv()
     gwi[...] = jnp.zeros_like(gwi)
@@ -255,75 +267,99 @@
     lax.fori_loop(0, NBLOCKS, pointwise, 0)
 
     hd = halo(dcb, hd_row, hd_col, hd_cor, hd_send, hd_recv)
-    save_mixed = pltpu.make_async_copy(mixed, mixed_out, local_sem.at[4])
-    save_mixed.start()
+    saves = []
+
+    def save_part(src, dst):
+        copy = pltpu.make_async_copy(src, dst, out_sem.at[len(saves)])
+        copy.start()
+        saves.append(copy)
+
+    save_part(mixed, mixed_out)
 
     for q in range(4):
         turned = gwo[:, q * 128 : (q + 1) * 128].T
         for u in range(16):
-            tile = turned[u * 8 : (u + 1) * 8]
-            at = q * 4 + u // 4
-            grads[at, 8 + 2 * (u % 4)] = tile[0:4]
-            grads[at, 9 + 2 * (u % 4)] = tile[4:8]
-
-    def deal(p, _):
-        rows = gwi[pl.ds(pl.multiple_of(p * 8, 8), 8), :]
-        for q in range(4):
-            tile = rows[:, q * 128 : (q + 1) * 128]
-            grads[p, 2 * q] = tile[0:4]
-            grads[p, 2 * q + 1] = tile[4:8]
-        return 0
-
-    lax.fori_loop(0, XY, deal, 0)
-
-    def copy_1(k):
-        peer = (me + k) % XY
+            p, at = q * 4 + u // 4, u % 4
+            grads[1, p * 8 : (p + 1) * 8, at * 128 : (at + 1) * 128] = turned[u * 8 : (u + 1) * 8]
+    grads[0] = gwi[...]
+
+    def remote(src, dst, sem, device):
         return pltpu.make_async_remote_copy(
-            src_ref=grads.at[peer], dst_ref=r1.at[k], send_sem=s1_send.at[k], recv_sem=s1_recv.at[k],
-            device_id=xy_id(peer), device_id_type=MESH,
+            src_ref=src, dst_ref=dst, send_sem=x_send.at[sem], recv_sem=x_recv.at[sem], device_id=device, device_id_type=MESH
         )
 
-    def copy_1s(k):
-        peer = (me + k) % XY
-        return pltpu.make_async_remote_copy(
-            src_ref=small.at[peer], dst_ref=r1s.at[k], send_sem=s1s_send.at[k], recv_sem=s1s_recv.at[k],
-            device_id=xy_id(peer), device_id_type=MESH,
-        )
-
-    def copy_2(k):
-        peer = (mr + k) % NR
-        return pltpu.make_async_remote_copy(
-            src_ref=s2.at[peer], dst_ref=r2.at[mr], send_sem=s2_send.at[k], recv_sem=s2_recv.at[k],
-            device_id=row_id(peer), device_id_type=MESH,
-        )
-
-    def copy_3(k):
-        peer = (mr + k) % NR
-        return pltpu.make_async_remote_copy(
-            src_ref=a4.at[mc, mr], dst_ref=a4.at[mc, mr], send_sem=s3_send.at[k], recv_sem=s3_recv.at[k],
-            device_id=row_id(peer), device_id_type=MESH,
-        )
-
-    def copy_4(k):
-        return pltpu.make_async_remote_copy(
-            src_ref=a4.at[mc], dst_ref=a4.at[mc], send_sem=s4_send.at[k], recv_sem=s4_recv.at[k],
-            device_id=(mf, mr, (mc + k) % NC), device_id_type=MESH,
-        )
-
-    def copy_4s(k):
-        return pltpu.make_async_remote_copy(
-            src_ref=sa.at[me], dst_ref=sa.at[me], send_sem=s4s_send.at[k], recv_sem=s4s_recv.at[k],
-            device_id=xy_id((me + k) % XY), device_id_type=MESH,
-        )
-
-    def each(count, act):
-        def step(k, _):
-            act(k)
+    def start(copies):
+        for copy in copies:
+            copy.start()
+
+    def arrived(ref, sem):
+        pltpu.make_async_copy(ref, ref, x_recv.at[sem]).wait()
+
+    def left_here(ref, sem):
+        pltpu.make_async_copy(ref, ref, x_send.at[sem]).wait()
+
+    far_xy = (10, 6, 2, 14, 8, 9, 11, 7, 12, 4, 5, 13, 3, 1, 15)
+    far_z = (4, 3, 5, 2, 6, 1, 7)
+    far_rows = (8, 7, 9, 6, 10, 5, 11, 4, 12, 3, 13, 2, 14, 1, 15)
+    far_cols = (6, 2, 4, 5, 7, 3, 1)
+
+    start([remote(grads.at[1 - core], from_core, 0, (mf, other, mc))])
+
+    def send_pair():
+        arrived(from_core, 0)
+
+        def add(p, _):
+            rows = pl.ds(pl.multiple_of(p * 8, 8), 8)
+            pair[rows, :] = grads[core, rows, :] + from_core[rows, :]
             return 0
 
-        lax.fori_loop(1, count, step, 0)
-
-    each(XY, lambda k: copy_1(k).start())
+        lax.fori_loop(0, XY, add, 0)
+        copies = []
+        for k in far_xy:
+            peer = (me + k) % XY
+            rows = pl.ds(pl.multiple_of(peer * 8, 8), 8)
+            copies.append(remote(pair.at[rows], r1.at[k - 1], 1, xy_id(peer)))
+        start(copies)
+
+    def send_sums():
+        arrived(r1, 1)
+        total = pair[pl.ds(pl.multiple_of(me * 8, 8), 8), :]
+        for k in range(XY - 1):
+            total = total + r1[k]
+        r2[mz] = total
+        start([remote(r2.at[mz], r2.at[mz], 2, row_id((mr + 2 * k) % NR)) for k in far_z])
+
+    def send_result():
+        arrived(r2.at[pl.ds(0, NR // 2 - 1)], 2)
+        total = r2[0]
+        for z in range(1, NR // 2):
+            total = total + r2[z]
+        a4[core, mc] = total
+        copies = []
+        for k in far_cols:
+            for row in (other, mr):
+                copies.append(remote(a4.at[core, mc], a4.at[core, mc], 3, (mf, row, (mc + k) % NC)))
+        copies.append(remote(a4.at[core, mc], a4.at[core, mc], 3, (mf, other, mc)))
+        start(copies)
+
+    def send_small():
+        start([remote(small.at[(me + k) % XY], r1s.at[k - 1], 4, xy_id((me + k) % XY)) for k in far_xy])
+
+    def send_small_sums():
+        arrived(r1s, 4)
+        total = small[me]
+        for k in range(XY - 1):
+            total = total + r1s[k]
+        r2s[mr] = total
+        start([remote(r2s.at[mr], r2s.at[mr], 5, row_id((mr + k) % NR)) for k in far_rows])
+
+    def send_small_result():
+        arrived(r2s.at[pl.ds(0, NR - 1)], 5)
+        total = r2s[0]
+        for r in range(1, NR):
+            total = total + r2s[r]
+        sa[me] = total
+        start([remote(sa.at[me], sa.at[me], 6, xy_id((me + k) % XY)) for k in far_xy])
 
     def tap_gradient(b):
         def step(wb, acc):
@@ -341,6 +377,8 @@
             kacc[pl.ds((a * 8 + b) * 8, 8), :] = acc[a]
 
     for b in range(7):
+        if b == 3:
+            send_pair()
         tap_gradient(b)
     for a in range(7):
         kacc[pl.ds((a * 8 + 7) * 8, 8), :] = jnp.zeros((8, C), F32)
@@ -353,7 +391,7 @@
     for q in range(4):
         small[14, pl.ds(q, 1), :] = jnp.sum(bacc[:, q * 128 : (q + 1) * 128], axis=0, keepdims=True)
     small[15] = jnp.broadcast_to(jnp.sum(gacc[...], axis=0, keepdims=True), (4, C))
-    each(XY, lambda k: copy_1s(k).start())
+    send_small()
 
     for copy in hd:
         copy.wait_recv()
@@ -366,69 +404,45 @@
             cv[h, pl.ds(first, 8), :] = acc[h]
         return 0
 
-    lax.fori_loop(0, 8, image_gradient, 0)
-
-    each(XY, lambda k: copy_1(k).wait_recv())
-    each(XY, lambda k: copy_1s(k).wait_recv())
-    little = small[me]
-    for k in range(1, XY):
-        little = little + r1s[k]
-
-    def sum_1(r, _):
-        total = grads[me, r]
-        for k in range(1, XY):
-            total = total + r1[k, r]
-        s2[r, 0] = total
-        s2[r, 1] = little
-        return 0
-
-    lax.fori_loop(0, NR, sum_1, 0)
-    each(NR, lambda k: copy_2(k).start())
-    r2[mr] = s2[mr]
-
-    lax.fori_loop(8, 12, image_gradient, 0)
-
-    each(NR, lambda k: copy_2(k).wait_recv())
-    total = r2[0]
-    for s in range(1, NR):
-        total = total + r2[s]
-    a4[mc, mr] = total[0]
-    sa[me] = total[1]
-    each(NR, lambda k: copy_3(k).start())
-    each(XY, lambda k: copy_4s(k).start())
-
+    def finish(wb, _):
+        first = pl.multiple_of(wb * 16, 16)
+        columns = pl.ds(first, 16)
+        for h in range(RH):
+            dimg[h, columns, :] = (cot[h, columns, :].astype(F32) + cv[h, columns, :]).astype(BF16)
+        return 0
+
+    lax.fori_loop(0, 6, image_gradient, 0)
+    send_sums()
+    lax.fori_loop(6, 12, image_gradient, 0)
+    send_small_sums()
     lax.fori_loop(12, 16, image_gradient, 0)
-
-    each(NR, lambda k: copy_3(k).wait_recv())
-    each(NC, lambda k: copy_4(k).start())
-
-    def finish(r, _):
-        dimg[r] = (cot[r].astype(F32) + cv[r]).astype(BF16)
-        return 0
-
-    lax.fori_loop(0, RH, finish, 0)
-    save_grad = pltpu.make_async_copy(dimg, d_image_out, local_sem.at[5])
-    save_grad.start()
-
-    each(XY, lambda k: copy_4s(k).wait_recv())
-    for a in range(7):
-        g_k_out[a, pl.ds(0, 4), :] = sa[2 * a]
-        g_k_out[a, pl.ds(4, 3), :] = sa[2 * a + 1][0:3]
-    for q in range(4):
-        g_b_out[:, q * 128 : (q + 1) * 128] = sa[14, pl.ds(q, 1), :]
-    g_gain_out[...] = sa[15, pl.ds(0, 1), :]
-
-    each(NC, lambda k: copy_4(k).wait_recv())
+    lax.fori_loop(0, 8, finish, 0)
+    save_part(dimg, d_image_out)
+    send_result()
+    send_small_result()
+
+    arrived(r1, 3)
+    for j in range(NC):
+        save_part(a4.at[0, j], g_in_out.at[pl.ds(j * 8, 8)])
 
     def place(j, _):
         for q in range(4):
-            at = pl.multiple_of(j * 8, 8)
-            g_in_out[pl.ds(at, 8), q * 128 : (q + 1) * 128] = jnp.concatenate([a4[j, 2 * q], a4[j, 2 * q + 1]], axis=0)
             at = pl.multiple_of(j * 32 + q * 8, 8)
-            g_out_out[pl.ds(at, 8), :] = jnp.concatenate([a4[j, 8 + 2 * q], a4[j, 9 + 2 * q]], axis=0)
+            g_out[pl.ds(at, 8), :] = a4[1, j, :, q * 128 : (q + 1) * 128]
         return 0
 
     lax.fori_loop(0, NC, place, 0)
+    save_part(g_out, g_out_out)
+    arrived(sa.at[pl.ds(0, XY - 1)], 6)
+    for a in range(7):
+        g_k[a, pl.ds(0, 4), :] = sa[2 * a]
+        g_k[a, pl.ds(4, 3), :] = sa[2 * a + 1][0:3]
+    for q in range(4):
+        g_b[:, q * 128 : (q + 1) * 128] = sa[14, pl.ds(q, 1), :]
+    g_gain[...] = sa[15, pl.ds(0, 1), :]
+    save_part(g_k, g_k_out)
+    save_part(g_b, g_b_out)
+    save_part(g_gain, g_gain_out)
 
     for copy in hx:
         copy.wait_send()
@@ -436,33 +450,52 @@
         copy.wait_send()
     send_in.wait_send()
     send_out.wait_send()
-    each(XY, lambda k: copy_1(k).wait_send())
-    each(XY, lambda k: copy_1s(k).wait_send())
-    each(NR, lambda k: copy_2(k).wait_send())
-    each(NR, lambda k: copy_3(k).wait_send())
-    each(XY, lambda k: copy_4s(k).wait_send())
-    each(NC, lambda k: copy_4(k).wait_send())
-    save_mixed.wait()
-    save_grad.wait()
+    left_here(from_core, 0)
+    left_here(r1, 1)
+    left_here(r2.at[pl.ds(0, NR // 2 - 1)], 2)
+    left_here(r1, 3)
+    left_here(r1s, 4)
+    left_here(r2s.at[pl.ds(0, NR - 1)], 5)
+    left_here(sa.at[pl.ds(0, XY - 1)], 6)
+    for copy in saves:
+        copy.wait()
+
+
+def save(*refs):
+    sources, targets, sem = refs[:7], refs[7:14], refs[14]
+    copies = [pltpu.make_async_copy(src, dst, sem.at[i]) for i, (src, dst) in enumerate(zip(sources, targets))]
+    for copy in copies:
+        copy.start()
+    for copy in copies:
+        copy.wait()
 
 
 def on_device(
     image, dw_kernel, dw_bias, layer_norm_gain, layer_norm_bias, w_in, b_in, w_out, b_out, cotangent
 ):
-    vmem = pl.BlockSpec(memory_space=pltpu.VMEM)
-    hbm = pl.BlockSpec(memory_space=pl.ANY)
+    hbm = pl.BlockSpec(memory_space=pltpu.HBM)
     sem = pltpu.SemaphoreType.DMA
     scratch = [
         pltpu.VMEM((RH, CW, C), BF16),
         pltpu.VMEM((RH, CW, C), BF16),
+        pltpu.VMEM((HID // 2, C), F32),
+        pltpu.VMEM((1, HID), F32),
+        pltpu.VMEM((7, 7, C), F32),
+        pltpu.VMEM((1, C), F32),
+        pltpu.VMEM((RH, CW, C), BF16),
+        pltpu.VMEM((RH, CW, C), BF16),
+        pltpu.VMEM((7, 7, C), F32),
+        pltpu.VMEM((1, C), F32),
+        pltpu.VMEM((1, C), F32),
+        pltpu.VMEM((1, C), F32),
+        pltpu.VMEM((1, HID), F32),
+        pltpu.VMEM((1, C), F32),
         pltpu.VMEM((RH + 6, CW + 16, C), F32),
         pltpu.VMEM((RH + 6, CW + 16, C), F32),
         pltpu.VMEM((RH, CW, C), F32),
         pltpu.VMEM((56, 8, C), F32),
         pltpu.VMEM((C, HID), BF16),
         pltpu.VMEM((HID, C), BF16),
-        pltpu.VMEM((RH, CW, C), BF16),
-        pltpu.VMEM((RH, CW, C), BF16),
         pltpu.VMEM((RH, CW, C), BF16),
         pltpu.VMEM((C, HID), F32),
         pltpu.VMEM((C, HID), F32),
@@ -477,38 +510,50 @@
             pltpu.VMEM((4, 3, 16, C), BF16),
         ]
     scratch += [
-        pltpu.VMEM((XY, NR, 4, C), F32),
-        pltpu.VMEM((XY, NR, 4, C), F32),
+        pltpu.VMEM((2, C, HID), F32),
+        pltpu.VMEM((C, HID), F32),
+        pltpu.VMEM((C, HID), F32),
+        pltpu.VMEM((XY - 1, 8, HID), F32),
+        pltpu.VMEM((NR // 2, 8, HID), F32),
+        pltpu.VMEM((2, NC, 8, HID), F32),
         pltpu.VMEM((XY, 4, C), F32),
+        pltpu.VMEM((XY - 1, 4, C), F32),
+        pltpu.VMEM((NR, 4, C), F32),
         pltpu.VMEM((XY, 4, C), F32),
-        pltpu.VMEM((NR, 2, 4, C), F32),
-        pltpu.VMEM((NR, 2, 4, C), F32),
-        pltpu.VMEM((NC, NR, 4, C), F32),
-        pltpu.VMEM((XY, 4, C), F32),
-        sem((6,)), sem((2,)), sem((2,)), sem((8,)), sem((8,)), sem((8,)), sem((8,)),
-    ] + [sem((16,)) for _ in range(12)]
+        sem((10,)), sem((2,)), sem((2,)), sem((8,)), sem((8,)), sem((8,)), sem((8,)), sem((7,)), sem((7,)), sem((14,)),
+    ]
+    shapes = (
+        jax.ShapeDtypeStruct((RH, CW, C), BF16),
+        jax.ShapeDtypeStruct((RH, CW, C), BF16),
+        jax.ShapeDtypeStruct((C // 2, HID), F32),
+        jax.ShapeDtypeStruct((HID // 2, C), F32),
+        jax.ShapeDtypeStruct((1, HID), F32),
+        jax.ShapeDtypeStruct((7, 7, C), F32),
+        jax.ShapeDtypeStruct((1, C), F32),
+    )
     outs = pl.pallas_call(
         kernel,
-        out_shape=(
-            jax.ShapeDtypeStruct((RH, CW, C), BF16),
-            jax.ShapeDtypeStruct((RH, CW, C), BF16),
-            jax.ShapeDtypeStruct((C // 2, HID), F32),
-            jax.ShapeDtypeStruct((HID // 2, C), F32),
-            jax.ShapeDtypeStruct((1, HID), F32),
-            jax.ShapeDtypeStruct((7, 7, C), F32),
-            jax.ShapeDtypeStruct((1, C), F32),
-        ),
-        in_specs=[hbm, vmem, vmem, vmem, vmem, hbm, vmem, hbm, vmem, hbm],
-        out_specs=(hbm, hbm, vmem, vmem, vmem, vmem, vmem),
+        out_shape=shapes,
+        in_specs=[hbm] * 10,
+        out_specs=(hbm,) * 7,
         scratch_shapes=scratch,
         compiler_params=pltpu.CompilerParams(
-            collective_id=0, has_side_effects=True, vmem_limit_bytes=48 * 1024 * 1024
+            collective_id=0, has_side_effects=True, vmem_limit_bytes=63 * 1024 * 1024
         ),
         name="convnext_block",
     )(
         image[0], dw_kernel, dw_bias.reshape(1, C), layer_norm_gain.reshape(1, C), layer_norm_bias.reshape(1, C),
         w_in, b_in.reshape(1, HID), w_out, b_out.reshape(1, C), cotangent[0],
     )
+    outs = pl.pallas_call(
+        save,
+        out_shape=shapes,
+        in_specs=[pl.BlockSpec(memory_space=pl.ANY)] * 7,
+        out_specs=(hbm,) * 7,
+        scratch_shapes=[sem((7,))],
+        compiler_params=pltpu.CompilerParams(vmem_limit_bytes=63 * 1024 * 1024),
+        name="save_outputs",
+    )(*outs)
     mixed, d_image, g_in, g_out, g_b, g_k, g_gain = outs
     return (mixed[None], d_image[None], g_in, g_out, g_b.reshape(HID), g_k, g_gain.reshape(C))
 

time: 67.6 us -> 91.5 us (1.35)
  Pallas kernels: 56.7 us -> 90.8 us
  local copies, waits for them, and re-layouts: 9.78 us -> 0 us
    pallas_call x1 -> x2, Pallas kernels: 56.7 us -> 90.8 us  [the longest x1 49.1 us: on_device(): pl.pallas_call(kernel, out_shape=shapes, in_specs=[hbm] * 10, out_specs=(...]
    unnamed x27 -> x0, local copies, waits for them, and re-layouts: 9.78 us -> none
where the time goes in v2:
time: 91.5 us; the launch traced here: 91.4 us
  Pallas kernels  90.8 us (99%)
    pallas_call x1, Pallas kernels, on_device(): pl.pallas_call(kernel, out_shape=shapes, in_specs=[hbm] * 10, out_specs=(...  49.1 us
    pallas_call x1, Pallas kernels, on_device(): pl.pallas_call(save, out_shape=shapes, in_specs=[pl.BlockSpec(memory_spac...  41.7 us

profile of v2, /device:TPU:1, one launch (start us, length us, event | category | flops | bytes accessed | tf_op | source)
XLA Modules:
  0.0 91.4 jit_solution(15533869497224424152)
XLA Ops:
  0.6 49.1 %convnext_block.1 = (bf16[16,128,128]{2,1,0:T(8,128)(2,1)}, bf16[16,128,128]{2,1,0:T(8,128)(2,1)}, f32[64,512]{1,0:T(8,128)}, f32[256,128]{1,0:T(8,128)}, f32[1,...) custom-call(bf16[16,128,128]{2,1,0:T(8,128)(2,1)} %bitcast.11, f32[7,7,128]{2,1,0:T(8,128)} %dw_kernel_in.1, ...), custom_call_target="tpu_custom_call" | custom-call | tf_op jit(solution)/shard_map/convnext_block/pallas_call | solution.py:534
  49.7 41.7 %save_outputs.1 = (bf16[16,128,128]{2,1,0:T(8,128)(2,1)}, bf16[16,128,128]{2,1,0:T(8,128)(2,1)}, f32[64,512]{1,0:T(8,128)}, f32[256,128]{1,0:T(8,128)}, f32[1,51...) custom-call(bf16[16,128,128]{2,1,0:T(8,128)(2,1)} %get-tuple-element.21.refs_0_, ...), custom_call_target="tpu_custom_call" | custom-call | tf_op jit(solution)/shard_map/save_outputs/pallas_call | solution.py:548

commit v3 on v2

--- a/solution.py
+++ b/solution.py
@@ -23,8 +23,7 @@
 XY = 16
 NR = 16
 NC = 8
-BLOCK = 256
-NBLOCKS = RH * CW // BLOCK
+PIX = RH * CW
 
 NT = (((1,), (1,)), ((), ()))
 TN = (((0,), (0,)), ((), ()))
@@ -48,7 +47,7 @@
     image, dw_kernel_in, dw_bias_in, gain_in, bias_in, w_in, b_in_in, w_out, b_out_in, cotangent,
     mixed_out, d_image_out, g_in_out, g_out_out, g_b_out, g_k_out, g_gain_out,
     mixed, dimg, g_out, g_b, g_k, g_gain, img, cot, dw_kernel, dw_bias, gain, bias, b_in, b_out, xp, dp, cv, kb, win, wout, dcb,
-    gwi, gwo, bacc, gacc, kacc,
+    bacc, gacc, kacc,
     hx_row, hx_col, hx_cor, hd_row, hd_col, hd_cor,
     grads, from_core, pair, r1, r2, a4, small, r1s, r2s, sa,
     local_sem, w_send, w_recv, hx_send, hx_recv, hd_send, hd_recv, x_send, x_recv, out_sem,
@@ -216,55 +215,66 @@
         loads[i].wait()
     send_in.wait_recv()
     send_out.wait_recv()
-    gwi[...] = jnp.zeros_like(gwi)
-    gwo[...] = jnp.zeros_like(gwo)
-    bacc[...] = jnp.zeros_like(bacc)
-    gacc[...] = jnp.zeros_like(gacc)
-    rows_per = BLOCK // CW
-
-    def pointwise(i, _):
-        r0 = i * rows_per
-        conv = cv[pl.ds(r0, rows_per)].reshape(BLOCK, C)
-        center = jnp.mean(conv, axis=-1, keepdims=True)
-        spread = conv - center
-        rstd = lax.rsqrt(jnp.mean(spread * spread, axis=-1, keepdims=True) + norm_eps)
-        xhat = spread * rstd
-        normed = (xhat * gain[...] + bias[...]).astype(BF16)
-        up_b = cot[pl.ds(r0, rows_per)].reshape(BLOCK, C)
-        out_sum = jnp.zeros((BLOCK, C), F32)
-        dn = jnp.zeros((BLOCK, C), F32)
-        half = HID // 2
-        for j in range(2):
-            cols = slice(j * half, (j + 1) * half)
-            pre = jnp.dot(normed, win[:, cols], preferred_element_type=F32) + b_in[:, cols]
-            square = pre * pre
-            tanh_val = jnp.tanh(pre * (gelu_coef + (gelu_coef * cubic_coef) * square))
-            half_gate = 0.5 + 0.5 * tanh_val
-            hidden = (pre * half_gate).astype(BF16)
-            slope = half_gate + (pre * (0.5 - 0.5 * tanh_val * tanh_val)) * (
-                gelu_coef + (3.0 * gelu_coef * cubic_coef) * square
-            )
-            d_hidden = lax.dot_general(up_b, wout[cols, :], NT, preferred_element_type=F32)
-            d_wide = d_hidden * slope
-            d_pre = d_wide.astype(BF16)
-            bacc[:, cols] += jnp.sum(d_wide.reshape(BLOCK // 8, 8, half), axis=0)
-            out_sum = out_sum + jnp.dot(hidden, wout[cols, :], preferred_element_type=F32)
-            dn = dn + lax.dot_general(d_pre, win[:, cols], NT, preferred_element_type=F32)
-            gwi[:, cols] += lax.dot_general(normed, d_pre, TN, preferred_element_type=F32)
-            gwo[:, cols] += lax.dot_general(up_b, hidden, TN, preferred_element_type=F32)
-        field = img[pl.ds(r0, rows_per)].reshape(BLOCK, C).astype(F32)
-        mixed[pl.ds(r0, rows_per)] = (field + out_sum + b_out[...]).astype(BF16).reshape(rows_per, CW, C)
-        gacc[...] += jnp.sum((dn * xhat).reshape(BLOCK // 8, 8, C), axis=0)
-        q = dn * gain[...]
-        d_conv = (
-            rstd * (q - jnp.mean(q, axis=-1, keepdims=True) - xhat * jnp.mean(q * xhat, axis=-1, keepdims=True))
-        ).astype(BF16)
-        d_rows = d_conv.reshape(rows_per, CW, C)
-        dcb[pl.ds(r0, rows_per)] = d_rows
-        dp[pl.ds(3 + r0, rows_per), pl.ds(8, CW), :] = d_rows.astype(F32)
-        return 0
-
-    lax.fori_loop(0, NBLOCKS, pointwise, 0)
+    def remote(src, dst, sem, device):
+        return pltpu.make_async_remote_copy(
+            src_ref=src, dst_ref=dst, send_sem=x_send.at[sem], recv_sem=x_recv.at[sem], device_id=device, device_id_type=MESH
+        )
+
+    def start(copies):
+        for copy in copies:
+            copy.start()
+
+    def arrived(ref, sem):
+        pltpu.make_async_copy(ref, ref, x_recv.at[sem]).wait()
+
+    def left_here(ref, sem):
+        pltpu.make_async_copy(ref, ref, x_send.at[sem]).wait()
+
+    far_xy = (10, 6, 2, 14, 8, 9, 11, 7, 12, 4, 5, 13, 3, 1, 15)
+    far_z = (4, 3, 5, 2, 6, 1, 7)
+    far_rows = (8, 7, 9, 6, 10, 5, 11, 4, 12, 3, 13, 2, 14, 1, 15)
+    far_cols = (6, 2, 4, 5, 7, 3, 1)
+
+    conv = cv[...].reshape(PIX, C)
+    center = jnp.mean(conv, axis=-1, keepdims=True)
+    spread = conv - center
+    rstd = lax.rsqrt(jnp.mean(spread * spread, axis=-1, keepdims=True) + norm_eps)
+    xhat = spread * rstd
+    normed = (xhat * gain[...] + bias[...]).astype(BF16)
+    upstream = cot[...].reshape(PIX, C)
+    pre = jnp.dot(normed, win[...], preferred_element_type=F32) + b_in[...]
+    square = pre * pre
+    tanh_val = jnp.tanh(pre * (gelu_coef + (gelu_coef * cubic_coef) * square))
+    half_gate = 0.5 + 0.5 * tanh_val
+    hidden = (pre * half_gate).astype(BF16)
+    slope = half_gate + (pre * (0.5 - 0.5 * tanh_val * tanh_val)) * (
+        gelu_coef + (3.0 * gelu_coef * cubic_coef) * square
+    )
+    d_wide = lax.dot_general(upstream, wout[...], NT, preferred_element_type=F32) * slope
+    d_pre = d_wide.astype(BF16)
+    bacc[...] = jnp.sum(d_wide.reshape(PIX // 8, 8, HID), axis=0)
+
+    grads[0] = lax.dot_general(normed, d_pre, TN, preferred_element_type=F32)
+    out_turned = lax.dot_general(upstream, hidden, TN, preferred_element_type=F32)
+    for q in range(4):
+        turned = out_turned[:, q * 128 : (q + 1) * 128].T
+        for u in range(16):
+            p, at = q * 4 + u // 4, u % 4
+            grads[1, p * 8 : (p + 1) * 8, at * 128 : (at + 1) * 128] = turned[u * 8 : (u + 1) * 8]
+    start([remote(grads.at[1 - core], from_core, 0, (mf, other, mc))])
+
+    out_sum = jnp.dot(hidden, wout[...], preferred_element_type=F32)
+    field = img[...].reshape(PIX, C).astype(F32)
+    mixed[...] = (field + out_sum + b_out[...]).astype(BF16).reshape(RH, CW, C)
+    dn = lax.dot_general(d_pre, win[...], NT, preferred_element_type=F32)
+    gacc[...] = jnp.sum((dn * xhat).reshape(PIX // 8, 8, C), axis=0)
+    q = dn * gain[...]
+    d_conv = (
+        rstd * (q - jnp.mean(q, axis=-1, keepdims=True) - xhat * jnp.mean(q * xhat, axis=-1, keepdims=True))
+    ).astype(BF16)
+    d_rows = d_conv.reshape(RH, CW, C)
+    dcb[...] = d_rows
+    dp[pl.ds(3, RH), pl.ds(8, CW), :] = d_rows.astype(F32)
 
     hd = halo(dcb, hd_row, hd_col, hd_cor, hd_send, hd_recv)
     saves = []
@@ -275,35 +285,6 @@
         saves.append(copy)
 
     save_part(mixed, mixed_out)
-
-    for q in range(4):
-        turned = gwo[:, q * 128 : (q + 1) * 128].T
-        for u in range(16):
-            p, at = q * 4 + u // 4, u % 4
-            grads[1, p * 8 : (p + 1) * 8, at * 128 : (at + 1) * 128] = turned[u * 8 : (u + 1) * 8]
-    grads[0] = gwi[...]
-
-    def remote(src, dst, sem, device):
-        return pltpu.make_async_remote_copy(
-            src_ref=src, dst_ref=dst, send_sem=x_send.at[sem], recv_sem=x_recv.at[sem], device_id=device, device_id_type=MESH
-        )
-
-    def start(copies):
-        for copy in copies:
-            copy.start()
-
-    def arrived(ref, sem):
-        pltpu.make_async_copy(ref, ref, x_recv.at[sem]).wait()
-
-    def left_here(ref, sem):
-        pltpu.make_async_copy(ref, ref, x_send.at[sem]).wait()
-
-    far_xy = (10, 6, 2, 14, 8, 9, 11, 7, 12, 4, 5, 13, 3, 1, 15)
-    far_z = (4, 3, 5, 2, 6, 1, 7)
-    far_rows = (8, 7, 9, 6, 10, 5, 11, 4, 12, 3, 13, 2, 14, 1, 15)
-    far_cols = (6, 2, 4, 5, 7, 3, 1)
-
-    start([remote(grads.at[1 - core], from_core, 0, (mf, other, mc))])
 
     def send_pair():
         arrived(from_core, 0)
@@ -372,7 +353,7 @@
                     acc[a] = acc[a] + value * grad[h]
             return tuple(acc)
 
-        acc = lax.fori_loop(0, CW // 8, step, tuple(jnp.zeros((8, C), F32) for _ in range(7)))
+        acc = lax.fori_loop(0, CW // 8, step, tuple(jnp.zeros((8, C), F32) for _ in range(7)), unroll=4)
         for a in range(7):
             kacc[pl.ds((a * 8 + b) * 8, 8), :] = acc[a]
 
@@ -462,11 +443,24 @@
 
 
 def save(*refs):
-    sources, targets, sem = refs[:7], refs[7:14], refs[14]
-    copies = [pltpu.make_async_copy(src, dst, sem.at[i]) for i, (src, dst) in enumerate(zip(sources, targets))]
-    for copy in copies:
+    sources, targets, held = refs[:7], refs[7:14], refs[14:21]
+    load_sem, save_sem = refs[21:]
+    parts = []
+    for src, dst, mid in zip(sources, targets, held):
+        if src.shape[0] == RH:
+            for at in range(0, RH, 4):
+                rows = pl.ds(at, 4)
+                parts.append((src.at[rows], dst.at[rows], mid.at[rows]))
+        else:
+            parts.append((src, dst, mid))
+    loads = [pltpu.make_async_copy(src, mid, load_sem.at[i]) for i, (src, _, mid) in enumerate(parts)]
+    saves = [pltpu.make_async_copy(mid, dst, save_sem.at[i]) for i, (_, dst, mid) in enumerate(parts)]
+    for copy in loads:
         copy.start()
-    for copy in copies:
+    for load, copy in zip(loads, saves):
+        load.wait()
+        copy.start()
+    for copy in saves:
         copy.wait()
 
 
@@ -497,8 +491,6 @@
         pltpu.VMEM((C, HID), BF16),
         pltpu.VMEM((HID, C), BF16),
         pltpu.VMEM((RH, CW, C), BF16),
-        pltpu.VMEM((C, HID), F32),
-        pltpu.VMEM((C, HID), F32),
         pltpu.VMEM((8, HID), F32),
         pltpu.VMEM((8, C), F32),
         pltpu.VMEM((448, C), F32),
@@ -550,7 +542,7 @@
         out_shape=shapes,
         in_specs=[pl.BlockSpec(memory_space=pl.ANY)] * 7,
         out_specs=(hbm,) * 7,
-        scratch_shapes=[sem((7,))],
+        scratch_shapes=[pltpu.VMEM(x.shape, x.dtype) for x in shapes] + [sem((13,)), sem((13,))],
         compiler_params=pltpu.CompilerParams(vmem_limit_bytes=63 * 1024 * 1024),
         name="save_outputs",
     )(*outs)

time: 91.5 us -> 48.4 us (0.53)
  Pallas kernels: 90.8 us -> 47.6 us
    pallas_call x1, Pallas kernels: 41.7 us -> 2.27 us  [on_device(): pl.pallas_call(save, out_shape=shapes, in_specs=[pl.BlockSpec(memory_spac...]
    pallas_call x1, Pallas kernels: 49.1 us -> 45.4 us  [on_device(): pl.pallas_call(kernel, out_shape=shapes, in_specs=[hbm] * 10, out_specs=(...]
where the time goes in v3:
time: 48.4 us; the launch traced here: 48.3 us
  Pallas kernels  47.6 us (98%)
  between operations  0.64 us (1%)
    pallas_call x1, Pallas kernels, on_device(): pl.pallas_call(kernel, out_shape=shapes, in_specs=[hbm] * 10, out_specs=(...  45.4 us
    pallas_call x1, Pallas kernels, on_device(): pl.pallas_call(save, out_shape=shapes, in_specs=[pl.BlockSpec(memory_spac...  2.27 us

profile of v3, /device:TPU:1, one launch (start us, length us, event | category | flops | bytes accessed | tf_op | source)
XLA Modules:
  0.0 48.3 jit_solution(6317016401074305130)
XLA Ops:
  0.6 45.4 %convnext_block.1 = (bf16[16,128,128]{2,1,0:T(8,128)(2,1)}, bf16[16,128,128]{2,1,0:T(8,128)(2,1)}, f32[64,512]{1,0:T(8,128)}, f32[256,128]{1,0:T(8,128)}, f32[1,...) custom-call(bf16[16,128,128]{2,1,0:T(8,128)(2,1)} %bitcast.11, f32[7,7,128]{2,1,0:T(8,128)} %dw_kernel_in.1, ...), custom_call_target="tpu_custom_call" | custom-call | tf_op jit(solution)/shard_map/convnext_block/pallas_call | solution.py:526
  46.0 2.3 %save_outputs.1 = (bf16[16,128,128]{2,1,0:T(8,128)(2,1)}, bf16[16,128,128]{2,1,0:T(8,128)(2,1)}, f32[64,512]{1,0:T(8,128)}, f32[256,128]{1,0:T(8,128)}, f32[1,51...) custom-call(bf16[16,128,128]{2,1,0:T(8,128)(2,1)} %get-tuple-element.21.refs_0_, ...), custom_call_target="tpu_custom_call" | custom-call | tf_op jit(solution)/shard_map/save_outputs/pallas_call | solution.py:540

commit v4 on v3

--- a/solution.py
+++ b/solution.py
@@ -45,12 +45,12 @@
 
 def kernel(
     image, dw_kernel_in, dw_bias_in, gain_in, bias_in, w_in, b_in_in, w_out, b_out_in, cotangent,
-    mixed_out, d_image_out, g_in_out, g_out_out, g_b_out, g_k_out, g_gain_out,
-    mixed, dimg, g_out, g_b, g_k, g_gain, img, cot, dw_kernel, dw_bias, gain, bias, b_in, b_out, xp, dp, cv, kb, win, wout, dcb,
+    mixed, dimg, g_in, g_out, g_b, g_k, g_gain,
+    img, cot, dw_kernel, dw_bias, gain, bias, b_in, b_out, xp, dp, cv, kb, win, wout, dcb,
     bacc, gacc, kacc,
-    hx_row, hx_col, hx_cor, hd_row, hd_col, hd_cor,
+    wide, hx_side, hd_side, hx_row, hx_col, hx_cor, hd_row, hd_col, hd_cor,
     grads, from_core, pair, r1, r2, a4, small, r1s, r2s, sa,
-    local_sem, w_send, w_recv, hx_send, hx_recv, hd_send, hd_recv, x_send, x_recv, out_sem,
+    local_sem, w_send, w_recv, hx_send, hx_recv, hd_send, hd_recv, x_send, x_recv,
 ):
     mf = lax.axis_index("fsdp")
     mr = lax.axis_index("rows")
@@ -126,15 +126,26 @@
             cv[h, pl.ds(first, 8), :] = acc[h]
         return 0
 
+    def pack_sides(padded, wide, packed):
+        def row(r, _):
+            for j in range(3):
+                wide[0, j, pl.ds(r, 1), :] = padded[3 + r, pl.ds(CW + 5 + j, 1), :]
+                wide[1, j, pl.ds(r, 1), :] = padded[3 + r, pl.ds(8 + j, 1), :]
+            return 0
+
+        lax.fori_loop(0, RH, row, 0)
+        packed[...] = wide[...].astype(BF16)
+
+    pack_sides(xp, wide, hx_side)
     lax.fori_loop(1, 4, conv_inner, 0)
     pl.semaphore_wait(barrier, 2 + NC - 1 + XY - 1 + NR - 1)
 
-    def halo(source, rows_buf, col_buf, cor_buf, send, recv):
+    def halo(source, sides, rows_buf, col_buf, cor_buf, send, recv):
         plan = [
             (source.at[pl.ds(RH - 3, 3)], rows_buf.at[0], (mf, down, mc)),
             (source.at[pl.ds(0, 3)], rows_buf.at[1], (mf, up, mc)),
-            (source.at[:, pl.ds(CW - 16, 16)], col_buf.at[0], (mf, mr, right)),
-            (source.at[:, pl.ds(0, 16)], col_buf.at[1], (mf, mr, left)),
+            (sides.at[0], col_buf.at[0], (mf, mr, right)),
+            (sides.at[1], col_buf.at[1], (mf, mr, left)),
             (source.at[pl.ds(RH - 3, 3), pl.ds(CW - 16, 16)], cor_buf.at[0], (mf, down, right)),
             (source.at[pl.ds(RH - 3, 3), pl.ds(0, 16)], cor_buf.at[1], (mf, down, left)),
             (source.at[pl.ds(0, 3), pl.ds(CW - 16, 16)], cor_buf.at[2], (mf, up, right)),
@@ -154,7 +165,7 @@
     has_left = jnp.where(mc > 0, 1.0, 0.0).astype(F32)
     has_right = jnp.where(mc < NC - 1, 1.0, 0.0).astype(F32)
 
-    def unpack_halo(padded, rows_buf, col_buf, cor_buf):
+    def unpack_halo(padded, wide, rows_buf, col_buf, cor_buf):
         for i in range(3):
             padded[i, pl.ds(8, CW), :] = rows_buf[0, i].astype(F32) * has_up
             padded[RH + 3 + i, pl.ds(8, CW), :] = rows_buf[1, i].astype(F32) * has_down
@@ -163,14 +174,18 @@
             padded[RH + 3 + i, pl.ds(0, 8), :] = cor_buf[2, i].astype(F32)[8:16] * (has_down * has_left)
             padded[RH + 3 + i, pl.ds(CW + 8, 8), :] = cor_buf[3, i].astype(F32)[0:8] * (has_down * has_right)
 
+        wide[0] = col_buf[0].astype(F32) * has_left
+        wide[1] = col_buf[1].astype(F32) * has_right
+
         def side(r, _):
-            padded[3 + r, pl.ds(0, 8), :] = col_buf[0, r].astype(F32)[8:16] * has_left
-            padded[3 + r, pl.ds(CW + 8, 8), :] = col_buf[1, r].astype(F32)[0:8] * has_right
+            for j in range(3):
+                padded[3 + r, pl.ds(5 + j, 1), :] = wide[0, j, pl.ds(r, 1), :]
+                padded[3 + r, pl.ds(CW + 8 + j, 1), :] = wide[1, j, pl.ds(r, 1), :]
             return 0
 
         lax.fori_loop(0, RH, side, 0)
 
-    hx = halo(image, hx_row, hx_col, hx_cor, hx_send, hx_recv)
+    hx = halo(image, hx_side, hx_row, hx_col, hx_cor, hx_send, hx_recv)
     partner = (1 - mf, mr, mc)
     send_in = pltpu.make_async_remote_copy(
         src_ref=w_in, dst_ref=win.at[pl.ds(mf * 64, 64)], send_sem=w_send.at[0], recv_sem=w_recv.at[0],
@@ -187,7 +202,7 @@
 
     for copy in hx:
         copy.wait_recv()
-    unpack_halo(xp, hx_row, hx_col, hx_cor)
+    unpack_halo(xp, wide, hx_row, hx_col, hx_cor)
 
     def conv_edge(wb, _):
         first = pl.multiple_of(wb * 8, 8)
@@ -263,9 +278,6 @@
             grads[1, p * 8 : (p + 1) * 8, at * 128 : (at + 1) * 128] = turned[u * 8 : (u + 1) * 8]
     start([remote(grads.at[1 - core], from_core, 0, (mf, other, mc))])
 
-    out_sum = jnp.dot(hidden, wout[...], preferred_element_type=F32)
-    field = img[...].reshape(PIX, C).astype(F32)
-    mixed[...] = (field + out_sum + b_out[...]).astype(BF16).reshape(RH, CW, C)
     dn = lax.dot_general(d_pre, win[...], NT, preferred_element_type=F32)
     gacc[...] = jnp.sum((dn * xhat).reshape(PIX // 8, 8, C), axis=0)
     q = dn * gain[...]
@@ -276,15 +288,8 @@
     dcb[...] = d_rows
     dp[pl.ds(3, RH), pl.ds(8, CW), :] = d_rows.astype(F32)
 
-    hd = halo(dcb, hd_row, hd_col, hd_cor, hd_send, hd_recv)
-    saves = []
-
-    def save_part(src, dst):
-        copy = pltpu.make_async_copy(src, dst, out_sem.at[len(saves)])
-        copy.start()
-        saves.append(copy)
-
-    save_part(mixed, mixed_out)
+    pack_sides(dp, wide, hd_side)
+    hd = halo(dcb, hd_side, hd_row, hd_col, hd_cor, hd_send, hd_recv)
 
     def send_pair():
         arrived(from_core, 0)
@@ -374,9 +379,13 @@
     small[15] = jnp.broadcast_to(jnp.sum(gacc[...], axis=0, keepdims=True), (4, C))
     send_small()
 
+    out_sum = jnp.dot(hidden, wout[...], preferred_element_type=F32)
+    field = img[...].reshape(PIX, C).astype(F32)
+    mixed[...] = (field + out_sum + b_out[...]).astype(BF16).reshape(RH, CW, C)
+
     for copy in hd:
         copy.wait_recv()
-    unpack_halo(dp, hd_row, hd_col, hd_cor)
+    unpack_halo(dp, wide, hd_row, hd_col, hd_cor)
 
     def image_gradient(wb, _):
         first = pl.multiple_of(wb * 8, 8)
@@ -398,22 +407,18 @@
     send_small_sums()
     lax.fori_loop(12, 16, image_gradient, 0)
     lax.fori_loop(0, 8, finish, 0)
-    save_part(dimg, d_image_out)
     send_result()
     send_small_result()
 
     arrived(r1, 3)
-    for j in range(NC):
-        save_part(a4.at[0, j], g_in_out.at[pl.ds(j * 8, 8)])
-
     def place(j, _):
         for q in range(4):
             at = pl.multiple_of(j * 32 + q * 8, 8)
             g_out[pl.ds(at, 8), :] = a4[1, j, :, q * 128 : (q + 1) * 128]
+        g_in[pl.ds(pl.multiple_of(j * 8, 8), 8), :] = a4[0, j]
         return 0
 
     lax.fori_loop(0, NC, place, 0)
-    save_part(g_out, g_out_out)
     arrived(sa.at[pl.ds(0, XY - 1)], 6)
     for a in range(7):
         g_k[a, pl.ds(0, 4), :] = sa[2 * a]
@@ -421,9 +426,6 @@
     for q in range(4):
         g_b[:, q * 128 : (q + 1) * 128] = sa[14, pl.ds(q, 1), :]
     g_gain[...] = sa[15, pl.ds(0, 1), :]
-    save_part(g_k, g_k_out)
-    save_part(g_b, g_b_out)
-    save_part(g_gain, g_gain_out)
 
     for copy in hx:
         copy.wait_send()
@@ -438,29 +440,14 @@
     left_here(r1s, 4)
     left_here(r2s.at[pl.ds(0, NR - 1)], 5)
     left_here(sa.at[pl.ds(0, XY - 1)], 6)
-    for copy in saves:
-        copy.wait()
 
 
 def save(*refs):
-    sources, targets, held = refs[:7], refs[7:14], refs[14:21]
-    load_sem, save_sem = refs[21:]
-    parts = []
-    for src, dst, mid in zip(sources, targets, held):
-        if src.shape[0] == RH:
-            for at in range(0, RH, 4):
-                rows = pl.ds(at, 4)
-                parts.append((src.at[rows], dst.at[rows], mid.at[rows]))
-        else:
-            parts.append((src, dst, mid))
-    loads = [pltpu.make_async_copy(src, mid, load_sem.at[i]) for i, (src, _, mid) in enumerate(parts)]
-    saves = [pltpu.make_async_copy(mid, dst, save_sem.at[i]) for i, (_, dst, mid) in enumerate(parts)]
-    for copy in loads:
+    sources, targets, sem = refs[:7], refs[7:14], refs[14]
+    copies = [pltpu.make_async_copy(src, dst, sem.at[i]) for i, (src, dst) in enumerate(zip(sources, targets))]
+    for copy in copies:
         copy.start()
-    for load, copy in zip(loads, saves):
-        load.wait()
-        copy.start()
-    for copy in saves:
+    for copy in copies:
         copy.wait()
 
 
@@ -470,12 +457,6 @@
     hbm = pl.BlockSpec(memory_space=pltpu.HBM)
     sem = pltpu.SemaphoreType.DMA
     scratch = [
-        pltpu.VMEM((RH, CW, C), BF16),
-        pltpu.VMEM((RH, CW, C), BF16),
-        pltpu.VMEM((HID // 2, C), F32),
-        pltpu.VMEM((1, HID), F32),
-        pltpu.VMEM((7, 7, C), F32),
-        pltpu.VMEM((1, C), F32),
         pltpu.VMEM((RH, CW, C), BF16),
         pltpu.VMEM((RH, CW, C), BF16),
         pltpu.VMEM((7, 7, C), F32),
@@ -495,10 +476,15 @@
         pltpu.VMEM((8, C), F32),
         pltpu.VMEM((448, C), F32),
     ]
+    scratch += [
+        pltpu.VMEM((2, 3, RH, C), F32),
+        pltpu.VMEM((2, 3, RH, C), BF16),
+        pltpu.VMEM((2, 3, RH, C), BF16),
+    ]
     for _ in range(2):
         scratch += [
             pltpu.VMEM((2, 3, CW, C), BF16),
-            pltpu.VMEM((2, RH, 16, C), BF16),
+            pltpu.VMEM((2, 3, RH, C), BF16),
             pltpu.VMEM((4, 3, 16, C), BF16),
         ]
     scratch += [
@@ -512,7 +498,7 @@
         pltpu.VMEM((XY - 1, 4, C), F32),
         pltpu.VMEM((NR, 4, C), F32),
         pltpu.VMEM((XY, 4, C), F32),
-        sem((10,)), sem((2,)), sem((2,)), sem((8,)), sem((8,)), sem((8,)), sem((8,)), sem((7,)), sem((7,)), sem((14,)),
+        sem((10,)), sem((2,)), sem((2,)), sem((8,)), sem((8,)), sem((8,)), sem((8,)), sem((7,)), sem((7,)),
     ]
     shapes = (
         jax.ShapeDtypeStruct((RH, CW, C), BF16),
@@ -523,29 +509,29 @@
         jax.ShapeDtypeStruct((7, 7, C), F32),
         jax.ShapeDtypeStruct((1, C), F32),
     )
-    outs = pl.pallas_call(
-        kernel,
-        out_shape=shapes,
-        in_specs=[hbm] * 10,
-        out_specs=(hbm,) * 7,
-        scratch_shapes=scratch,
-        compiler_params=pltpu.CompilerParams(
-            collective_id=0, has_side_effects=True, vmem_limit_bytes=63 * 1024 * 1024
-        ),
-        name="convnext_block",
-    )(
+    operands = (
         image[0], dw_kernel, dw_bias.reshape(1, C), layer_norm_gain.reshape(1, C), layer_norm_bias.reshape(1, C),
         w_in, b_in.reshape(1, HID), w_out, b_out.reshape(1, C), cotangent[0],
     )
+    outs = pl.pallas_call(
+        kernel,
+        out_shape=tuple(pltpu.VMEM(x.shape, x.dtype) for x in shapes),
+        in_specs=[hbm] * 10,
+        out_specs=(pl.BlockSpec(memory_space=pltpu.VMEM),) * 7,
+        scratch_shapes=scratch,
+        compiler_params=pltpu.CompilerParams(
+            collective_id=0, has_side_effects=True, vmem_limit_bytes=48 * 1024 * 1024
+        ),
+        name="convnext_block",
+    )(*[pltpu.with_memory_space_constraint(x, pltpu.HBM) for x in operands])
     outs = pl.pallas_call(
         save,
         out_shape=shapes,
         in_specs=[pl.BlockSpec(memory_space=pl.ANY)] * 7,
         out_specs=(hbm,) * 7,
-        scratch_shapes=[pltpu.VMEM(x.shape, x.dtype) for x in shapes] + [sem((13,)), sem((13,))],
-        compiler_params=pltpu.CompilerParams(vmem_limit_bytes=63 * 1024 * 1024),
+        scratch_shapes=[sem((7,))],
         name="save_outputs",
-    )(*outs)
+    )(*[pltpu.with_memory_space_constraint(x, pltpu.VMEM) for x in outs])
     mixed, d_image, g_in, g_out, g_b, g_k, g_gain = outs
     return (mixed[None], d_image[None], g_in, g_out, g_b.reshape(HID), g_k, g_gain.reshape(C))
 

time: 48.4 us -> 45.2 us (0.934)
  Pallas kernels: 47.6 us -> 44.4 us
    pallas_call x1, Pallas kernels: 45.4 us -> 43.3 us  [on_device(): pl.pallas_call(kernel, out_shape=tuple((pltpu.VMEM(x.shape, x.dtype) for...]
    pallas_call x1, Pallas kernels: 2.27 us -> 1.11 us  [on_device(): pl.pallas_call(save, out_shape=shapes, in_specs=[pl.BlockSpec(memory_spac...]
where the time goes in v4:
time: 45.2 us; the launch traced here: 45.1 us
  Pallas kernels  44.4 us (98%)
  between operations  0.64 us (1%)
    pallas_call x1, Pallas kernels, on_device(): pl.pallas_call(kernel, out_shape=tuple((pltpu.VMEM(x.shape, x.dtype) for...  43.3 us
    pallas_call x1, Pallas kernels, on_device(): pl.pallas_call(save, out_shape=shapes, in_specs=[pl.BlockSpec(memory_spac...  1.11 us

profile of v4, /device:TPU:1, one launch (start us, length us, event | category | flops | bytes accessed | tf_op | source)
XLA Modules:
  0.0 45.1 jit_solution(15052838878661322419)
XLA Ops:
  0.6 43.3 %convnext_block.1 = (bf16[16,128,128]{2,1,0:T(8,128)(2,1)S(1)}, bf16[16,128,128]{2,1,0:T(8,128)(2,1)S(1)}, f32[64,512]{1,0:T(8,128)S(1)}, f32[256,128]{1,0:T(8,1...) custom-call(bf16[16,128,128]{2,1,0:T(8,128)(2,1)} %bitcast.11, ...), custom_call_target="tpu_custom_call" | custom-call | tf_op jit(solution)/shard_map/convnext_block/pallas_call | solution.py:516
  44.0 1.1 %save_outputs.1 = (bf16[16,128,128]{2,1,0:T(8,128)(2,1)}, bf16[16,128,128]{2,1,0:T(8,128)(2,1)}, f32[64,512]{1,0:T(8,128)}, f32[256,128]{1,0:T(8,128)}, f32[1,51...) custom-call(bf16[16,128,128]{2,1,0:T(8,128)(2,1)S(1)} %get-tuple-element.21.refs_0_, ...), custom_call_target="tpu_custom_call" | custom-call | tf_op jit(solution)/shard_map/save_outputs/pallas_call | solution.py:527

commit v5 on v4

--- a/solution.py
+++ b/solution.py
@@ -276,7 +276,6 @@
         for u in range(16):
             p, at = q * 4 + u // 4, u % 4
             grads[1, p * 8 : (p + 1) * 8, at * 128 : (at + 1) * 128] = turned[u * 8 : (u + 1) * 8]
-    start([remote(grads.at[1 - core], from_core, 0, (mf, other, mc))])
 
     dn = lax.dot_general(d_pre, win[...], NT, preferred_element_type=F32)
     gacc[...] = jnp.sum((dn * xhat).reshape(PIX // 8, 8, C), axis=0)
@@ -288,6 +287,7 @@
     dcb[...] = d_rows
     dp[pl.ds(3, RH), pl.ds(8, CW), :] = d_rows.astype(F32)
 
+    start([remote(grads.at[1 - core], from_core, 0, (mf, other, mc))])
     pack_sides(dp, wide, hd_side)
     hd = halo(dcb, hd_side, hd_row, hd_col, hd_cor, hd_send, hd_recv)
 
@@ -347,25 +347,29 @@
         sa[me] = total
         start([remote(sa.at[me], sa.at[me], 6, xy_id((me + k) % XY)) for k in far_xy])
 
-    def tap_gradient(b):
+    def tap_gradient(taps, unroll):
         def step(wb, acc):
             first = pl.multiple_of(wb * 8, 8)
             acc = list(acc)
             grad = [dp[3 + h, pl.ds(first + 8, 8), :] for h in range(RH)]
-            for row in range(RH + 6):
-                value = xp[row, pl.ds(first + 5 + b, 8), :]
-                for h, a in taps_all(row):
-                    acc[a] = acc[a] + value * grad[h]
+            for i, b in enumerate(taps):
+                for row in range(RH + 6):
+                    value = xp[row, pl.ds(first + 5 + b, 8), :]
+                    for h, a in taps_all(row):
+                        acc[i * 7 + a] = acc[i * 7 + a] + value * grad[h]
             return tuple(acc)
 
-        acc = lax.fori_loop(0, CW // 8, step, tuple(jnp.zeros((8, C), F32) for _ in range(7)), unroll=4)
-        for a in range(7):
-            kacc[pl.ds((a * 8 + b) * 8, 8), :] = acc[a]
-
-    for b in range(7):
-        if b == 3:
-            send_pair()
-        tap_gradient(b)
+        zero = jnp.zeros((8, C), F32)
+        acc = lax.fori_loop(0, CW // 8, step, (zero,) * (7 * len(taps)), unroll=unroll)
+        for i, b in enumerate(taps):
+            for a in range(7):
+                kacc[pl.ds((a * 8 + b) * 8, 8), :] = acc[i * 7 + a]
+
+    tap_gradient((0, 1), 2)
+    send_pair()
+    tap_gradient((2, 3), 2)
+    tap_gradient((4, 5), 2)
+    tap_gradient((6,), 4)
     for a in range(7):
         kacc[pl.ds((a * 8 + 7) * 8, 8), :] = jnp.zeros((8, C), F32)
     for a in range(7):
@@ -379,9 +383,6 @@
     small[15] = jnp.broadcast_to(jnp.sum(gacc[...], axis=0, keepdims=True), (4, C))
     send_small()
 
-    out_sum = jnp.dot(hidden, wout[...], preferred_element_type=F32)
-    field = img[...].reshape(PIX, C).astype(F32)
-    mixed[...] = (field + out_sum + b_out[...]).astype(BF16).reshape(RH, CW, C)
 
     for copy in hd:
         copy.wait_recv()
@@ -401,11 +402,14 @@
             dimg[h, columns, :] = (cot[h, columns, :].astype(F32) + cv[h, columns, :]).astype(BF16)
         return 0
 
-    lax.fori_loop(0, 6, image_gradient, 0)
+    lax.fori_loop(0, 4, image_gradient, 0)
     send_sums()
-    lax.fori_loop(6, 12, image_gradient, 0)
+    lax.fori_loop(4, 8, image_gradient, 0)
     send_small_sums()
-    lax.fori_loop(12, 16, image_gradient, 0)
+    lax.fori_loop(8, 16, image_gradient, 0)
+    out_sum = jnp.dot(hidden, wout[...], preferred_element_type=F32)
+    field = img[...].reshape(PIX, C).astype(F32)
+    mixed[...] = (field + out_sum + b_out[...]).astype(BF16).reshape(RH, CW, C)
     lax.fori_loop(0, 8, finish, 0)
     send_result()
     send_small_result()

time: 45.2 us -> 44.3 us (0.980)
  Pallas kernels: 44.4 us -> 43.5 us
    pallas_call x1, Pallas kernels: 43.3 us -> 42.4 us  [on_device(): pl.pallas_call(kernel, out_shape=tuple((pltpu.VMEM(x.shape, x.dtype) for...]
where the time goes in v5:
time: 44.3 us; the launch traced here: 44.2 us
  Pallas kernels  43.5 us (98%)
  between operations  0.64 us (1%)
    pallas_call x1, Pallas kernels, on_device(): pl.pallas_call(kernel, out_shape=tuple((pltpu.VMEM(x.shape, x.dtype) for...  42.4 us
    pallas_call x1, Pallas kernels, on_device(): pl.pallas_call(save, out_shape=shapes, in_specs=[pl.BlockSpec(memory_spac...  1.11 us

profile of v5, /device:TPU:1, one launch (start us, length us, event | category | flops | bytes accessed | tf_op | source)
XLA Modules:
  0.0 44.2 jit_solution(6291762507800416678)
XLA Ops:
  0.6 42.4 %convnext_block.1 = (bf16[16,128,128]{2,1,0:T(8,128)(2,1)S(1)}, bf16[16,128,128]{2,1,0:T(8,128)(2,1)S(1)}, f32[64,512]{1,0:T(8,128)S(1)}, f32[256,128]{1,0:T(8,1...) custom-call(bf16[16,128,128]{2,1,0:T(8,128)(2,1)} %bitcast.11, ...), custom_call_target="tpu_custom_call" | custom-call | tf_op jit(solution)/shard_map/convnext_block/pallas_call | solution.py:520
  43.1 1.1 %save_outputs.1 = (bf16[16,128,128]{2,1,0:T(8,128)(2,1)}, bf16[16,128,128]{2,1,0:T(8,128)(2,1)}, f32[64,512]{1,0:T(8,128)}, f32[256,128]{1,0:T(8,128)}, f32[1,51...) custom-call(bf16[16,128,128]{2,1,0:T(8,128)(2,1)S(1)} %get-tuple-element.21.refs_0_, ...), custom_call_target="tpu_custom_call" | custom-call | tf_op jit(solution)/shard_map/save_outputs/pallas_call | solution.py:531

commit v6 on v5

--- a/solution.py
+++ b/solution.py
@@ -407,12 +407,12 @@
     lax.fori_loop(4, 8, image_gradient, 0)
     send_small_sums()
     lax.fori_loop(8, 16, image_gradient, 0)
+    send_result()
+    send_small_result()
     out_sum = jnp.dot(hidden, wout[...], preferred_element_type=F32)
     field = img[...].reshape(PIX, C).astype(F32)
     mixed[...] = (field + out_sum + b_out[...]).astype(BF16).reshape(RH, CW, C)
     lax.fori_loop(0, 8, finish, 0)
-    send_result()
-    send_small_result()
 
     arrived(r1, 3)
     def place(j, _):

time: 44.3 us -> 44.1 us (level)
  no operation moved by 1% of the time
where the time goes in v6:
time: 44.1 us; the launch traced here: 44 us
  Pallas kernels  43.4 us (98%)
  between operations  0.64 us (1%)
    pallas_call x1, Pallas kernels, on_device(): pl.pallas_call(kernel, out_shape=tuple((pltpu.VMEM(x.shape, x.dtype) for...  42.3 us
    pallas_call x1, Pallas kernels, on_device(): pl.pallas_call(save, out_shape=shapes, in_specs=[pl.BlockSpec(memory_spac...  1.11 us

profile of v6, /device:TPU:1, one launch (start us, length us, event | category | flops | bytes accessed | tf_op | source)
XLA Modules:
  0.0 44.0 jit_solution(1256839422602603276)
XLA Ops:
  0.6 42.3 %convnext_block.1 = (bf16[16,128,128]{2,1,0:T(8,128)(2,1)S(1)}, bf16[16,128,128]{2,1,0:T(8,128)(2,1)S(1)}, f32[64,512]{1,0:T(8,128)S(1)}, f32[256,128]{1,0:T(8,1...) custom-call(bf16[16,128,128]{2,1,0:T(8,128)(2,1)} %bitcast.11, ...), custom_call_target="tpu_custom_call" | custom-call | tf_op jit(solution)/shard_map/convnext_block/pallas_call | solution.py:520
  42.9 1.1 %save_outputs.1 = (bf16[16,128,128]{2,1,0:T(8,128)(2,1)}, bf16[16,128,128]{2,1,0:T(8,128)(2,1)}, f32[64,512]{1,0:T(8,128)}, f32[256,128]{1,0:T(8,128)}, f32[1,51...) custom-call(bf16[16,128,128]{2,1,0:T(8,128)(2,1)S(1)} %get-tuple-element.21.refs_0_, ...), custom_call_target="tpu_custom_call" | custom-call | tf_op jit(solution)/shard_map/save_outputs/pallas_call | solution.py:531
